TPU v7x, 32 devices: a whole 2x2x4 slice. The times are simulated.
32 devices in a mesh: ctx: 8 (over y, x, core), exp: 4 (over z).
Axes of the slice: x: 2, y: 2, z: 4, core: 2. Of those that a mesh axis runs over, the one named last changes fastest.
Arguments:
- queries: bfloat16 [4, 512, 8192], P(None, 'ctx', 'exp'), may hold values from -2 to 2
- keys: bfloat16 [4, 512, 8192], P(None, 'ctx', 'exp'), may hold values from -2 to 2
- values: bfloat16 [4, 512, 8192], P(None, 'ctx', 'exp'), may hold values from -6 to 6
- decay_log: float32 [512, 64], P('ctx', 'exp'), may hold values from -0.9 to 0
- out_gate: bfloat16 [4, 512, 8192], P(None, 'ctx', 'exp'), may hold values from -6 to 6
- head_gain: float32 [8192], P('exp'), may hold values from 0.1 to 1.9
- out_weight: bfloat16 [8192, 6144], P('exp', 'ctx'), may hold values from -0.0625 to 0.0625
- stream: bfloat16 [4, 512, 6144], P(None, ('ctx', 'exp')), may hold values from -6 to 6
- norm_gain: float32 [6144], replicated, may hold values from 0.1 to 1.9
- expert_ids: int32 [32, 64, 2], P(('ctx', 'exp')), may hold values from 0 to 3, all different within a row; in each aligned block of 64 rows (0 to 63, 64 to 127, ..., all dimensions but the last counted through in order) at most 33 rows name the same one
- expert_share: float32 [32, 64, 2], P(('ctx', 'exp')), may hold values from 0.2 to 1
- w_gate: bfloat16 [4, 6144, 9216], P('exp', None, 'ctx'), may hold values from -0.078125 to 0.078125
- w_up: bfloat16 [4, 6144, 9216], P('exp', None, 'ctx'), may hold values from -0.078125 to 0.078125
- w_down: bfloat16 [4, 9216, 6144], P('exp', 'ctx'), may hold values from -0.0625 to 0.0625
Outputs:
- layer_out: bfloat16 [4, 512, 6144], P(None, ('ctx', 'exp'))
Inputs may be any that keep to these rules, and one draw needn't show every extreme that they name: `expert_ids`: within a routing group no expert takes more than 33 copies, some group gives one expert exactly 33, and the two picks of a token differ.
All inputs are finite; a program needn't handle non-finite values.
Results may differ from a plain program's by a relative error of at most 0.02.
Values may be sent and summed in bfloat16 or wider, within the bound.
No kernel may reach another device: no remote copies, remote signals or barrier semaphores. Data moves between devices by JAX's collectives and lax.ppermute only.
A program may use at most 192 MiB of HBM per device.

v0:
```python
import jax
import jax.numpy as jnp
from jax import lax
from jax.sharding import PartitionSpec as P


def carried_in(x, axis, join, neutral):
    place = lax.axis_index(axis)
    gathered = jax.tree.map(
        lambda a, kind: lax.all_gather(a.astype(kind), axis), x, (jnp.bfloat16, jnp.bfloat16)
    )
    state = jax.tree.map(lambda a, e: jnp.zeros_like(a) + jnp.asarray(e, a.dtype), x, neutral)

    def one(lap, state):
        return join(
            state,
            jax.tree.map(
                lambda a, own: lax.dynamic_index_in_dim(a, lap, 0, False).astype(own.dtype),
                gathered,
                x,
            ),
        )

    return lax.fori_loop(0, place, one, state)


def join_states(earlier, later):
    earlier_fade, earlier_state = earlier
    later_fade, later_state = later
    return (earlier_fade * later_fade, later_fade * earlier_state + later_state)


def body(
    queries,
    keys,
    values,
    decay_log,
    out_gate,
    head_gain,
    out_weight,
    stream,
    norm_gain,
    expert_ids,
    expert_share,
    w_gate,
    w_up,
    w_down,
):
    seq_count, block_len, head_width = queries.shape
    head_count = decay_log.shape[1]
    head_dim = head_width // head_count
    split_shape = (seq_count, block_len, head_count, head_dim)
    query_heads = queries.reshape(split_shape)
    key_heads = keys.reshape(split_shape)
    value_heads = values.reshape(split_shape)
    cumulative = jnp.cumsum(decay_log, axis=0)
    position = jnp.arange(block_len)
    causal = position[:, None] >= position[None, :]
    gap_log = cumulative[:, None, :] - cumulative[None, :, :]
    decay_grid = jnp.exp(jnp.where(causal[:, :, None], gap_log, -1e30))
    scores = jnp.einsum(
        "sihd,sjhd->sijh", query_heads, key_heads, preferred_element_type=jnp.float32
    )
    weights = (scores * decay_grid[None]).astype(jnp.bfloat16)
    within = jnp.einsum("sijh,sjhd->sihd", weights, value_heads, preferred_element_type=jnp.float32)
    block_end = cumulative[-1]
    keys_faded = jnp.exp(block_end[None, :] - cumulative)[None, :, :, None] * key_heads.astype(
        jnp.float32
    )
    local_state = jnp.einsum(
        "sjhd,sjhe->shde",
        keys_faded,
        value_heads.astype(jnp.float32),
        precision=lax.Precision.HIGHEST,
    )
    fading = jnp.broadcast_to(
        jnp.exp(block_end)[None, :, None, None], (seq_count, head_count, 1, 1)
    )
    identity = (jnp.ones_like(fading), jnp.zeros_like(local_state))
    incoming_fade, incoming = carried_in((fading, local_state), "ctx", join_states, identity)
    carried = jnp.exp(cumulative)[None, :, :, None] * jnp.einsum(
        "sihd,shde->sihe",
        query_heads.astype(jnp.float32),
        incoming,
        precision=lax.Precision.HIGHEST,
    )
    attended = within + carried
    mean_square = jnp.mean(attended * attended, axis=-1, keepdims=True)
    gate_act = jax.nn.sigmoid(out_gate.reshape(split_shape).astype(jnp.float32))
    gated = (
        attended
        * lax.rsqrt(mean_square + 1e-06)
        * head_gain.reshape(head_count, head_dim)
        * gate_act
    )
    mixed = gated.astype(jnp.bfloat16).reshape(seq_count, block_len, head_width)
    sub_len = stream.shape[1]
    model_width = stream.shape[2]
    exp_count = lax.axis_size("exp")
    tok_count = seq_count * sub_len
    ordered = (
        mixed.reshape(seq_count, exp_count, sub_len, head_width)
        .transpose(1, 0, 2, 3)
        .reshape(exp_count * tok_count, head_width)
    )
    full_weight = lax.all_gather(out_weight, "ctx", axis=1, tiled=True)
    chosen_rows = ordered
    projected = lax.psum_scatter(
        jnp.dot(chosen_rows, full_weight, preferred_element_type=jnp.float32).astype(jnp.bfloat16),
        "exp",
        scatter_dimension=0,
        tiled=True,
    ).astype(jnp.float32)
    residual_sum = stream.reshape(tok_count, model_width).astype(jnp.float32) + projected
    stream_square = jnp.mean(residual_sum * residual_sum, axis=-1, keepdims=True)
    normed = (residual_sum * lax.rsqrt(stream_square + 1e-06) * norm_gain).astype(jnp.bfloat16)
    expert_local = w_gate.shape[0]
    expert_count = expert_local * exp_count
    capacity = max(2, (2 * tok_count + expert_count - 1) // expert_count + 1)
    slot_total = expert_count * capacity
    picks = expert_ids.reshape(2 * tok_count)
    one_hot = (picks[:, None] == jnp.arange(expert_count, dtype=jnp.int32)[None, :]).astype(
        jnp.int32
    )
    ranking = jnp.sum(jnp.cumsum(one_hot, axis=0) * one_hot, axis=1) - 1
    slot_of = picks * capacity + ranking
    placing = slot_of[:, None] == jnp.arange(slot_total, dtype=jnp.int32)[None, :]
    copies = jnp.repeat(normed, 2, axis=0)
    dispatch = jnp.dot(
        placing.T.astype(jnp.bfloat16), copies, preferred_element_type=jnp.float32
    ).astype(jnp.bfloat16)
    dispatch = dispatch.reshape(exp_count, expert_local, capacity, model_width)
    received = lax.all_to_all(dispatch, "exp", split_axis=0, concat_axis=0, tiled=True)
    piece = lax.all_gather(received, "ctx", axis=0, tiled=True)
    gate_part = jnp.einsum("nemd,edh->nemh", piece, w_gate, preferred_element_type=jnp.float32)
    up_part = jnp.einsum("nemd,edh->nemh", piece, w_up, preferred_element_type=jnp.float32)
    hidden_units = (jax.nn.silu(gate_part) * up_part).astype(jnp.bfloat16)
    chosen_rows = hidden_units
    summed = lax.psum_scatter(
        jnp.einsum(
            "nemh,ehd->nemd", chosen_rows, w_down, preferred_element_type=jnp.float32
        ).astype(jnp.bfloat16),
        "ctx",
        scatter_dimension=0,
        tiled=True,
    )
    returned = lax.all_to_all(summed, "exp", split_axis=0, concat_axis=0, tiled=True).reshape(
        slot_total, model_width
    )
    weighting = jnp.where(placing, expert_share.reshape(2 * tok_count, 1), 0.0)
    weighting = jnp.sum(weighting.reshape(tok_count, 2, slot_total), axis=1)
    expert_mix = jnp.dot(weighting, returned.astype(jnp.float32), precision=lax.Precision.HIGHEST)
    result = (residual_sum + expert_mix).astype(jnp.bfloat16)
    return result.reshape(seq_count, sub_len, model_width)


def solution(mesh):
    return jax.shard_map(
        body,
        mesh=mesh,
        in_specs=(
            P(None, "ctx", "exp"),
            P(None, "ctx", "exp"),
            P(None, "ctx", "exp"),
            P("ctx", "exp"),
            P(None, "ctx", "exp"),
            P("exp"),
            P("exp", "ctx"),
            P(None, ("ctx", "exp"), None),
            P(),
            P(("ctx", "exp"), None, None),
            P(("ctx", "exp"), None, None),
            P("exp", None, "ctx"),
            P("exp", None, "ctx"),
            P("exp", "ctx", None),
        ),
        out_specs=P(None, ("ctx", "exp"), None),
        check_vma=False,
    )
```

profile of v0, /device:TPU:0, one launch (start us, length us, event | category | flops | bytes accessed | tf_op | source)
XLA Modules:
  0.0 701.5 jit_solution(17516358511841007772)
XLA Ops:
  6.5 0.9 copy.67
  7.8 6.2 fusion.30
  14.1 0.7 all-gather.6.cloned.1.call-update
  14.9 0.6 dynamic-slice
  16.4 15.3 %all-reduce = bf16[128]{0:T(256)(128)(2,1)S(1)} all-reduce(bf16[128]{0:T(256)(128)(2,1)S(1)} %dynamic-update-slice), channel_id=3, replica_groups=mesh['ctx'=8,'exp'=4] {'ctx'}, use_global_device_ids=true, to_apply=%add | all-reduce | flops 128 | bytes 512
  31.9 1.0 select_exponential_fusion
  32.9 2.6 fusion.33
  35.5 71.2 %all-gather.10.cloned.1.call-done = bf16[32,16,128,128]{3,2,1,0:T(8,128)(2,1)} async-done(((bf16[4,16,128,128]{3,2,1,0:T(8,128)(2,1)}), bf16[32,16,128,128]{3,2,1,0:T(8,128)(2,1)}) %all-gather.10.cloned.1.call-update) | async-done | bytes 16777232 | tf_op jit(solution)/shard_map/all_gather | solution.py:10
  106.7 2.5 broadcast_in_dim.28
  109.2 1.2 copy-done.4
  110.4 4.3 multiply_reduce_fusion
  114.8 0.8 fusion.24
  115.6 0.7 copy.78
  116.8 116.6 %all-gather.6.cloned.1.call-done = bf16[2048,6144]{1,0:T(8,128)(2,1)} async-done(((bf16[2048,768]{1,0:T(8,128)(2,1)}), bf16[2048,6144]{1,0:T(8,128)(2,1)}) %all-gather.6.cloned.1.call-update) | async-done | bytes 25165840 | tf_op jit(solution)/shard_map/all_gather | solution.py:106
  233.4 12.8 %convolution_convert_fusion = bf16[256,6144]{1,0:T(8,128)(2,1)} fusion(bf16[256,2048]{1,0:T(8,128)(2,1)S(1)} %bitcast.170, bf16[2048,6144]{1,0:T(8,128)(2,1)} %all-gather.6.cloned.1.call-done), kind=kOutput, calls=%fused_computation.11 | convolution fusion | flops 6444023808 | bytes 29360128 | tf_op jit(solution)/shard_map/dot_general | solution.py:109
  246.3 0.6 copy-done.8
  247.6 59.1 %reduce-scatter.3.cloned.1.call-done = bf16[64,6144]{1,0:T(8,128)(2,1)} async-done(((bf16[256,6144]{1,0:T(8,128)(2,1)}), bf16[64,6144]{1,0:T(8,128)(2,1)}) %reduce-scatter.3.cloned.1.call-update) | async-done | bytes 786448 | tf_op jit(solution)/shard_map/reduce_scatter | solution.py:108
  306.7 1.6 multiply_reduce_fusion.1
  308.6 0.9 broadcast_in_dim.32
  309.5 1.5 reshape.172
  311.1 3.3 convolution_convert_fusion.1
  314.4 2.0 reshape.173
  316.3 49.1 %all_to_all.10 = bf16[4,1,33,6144]{3,2,1,0:T(8,128)(2,1)} all-to-all(bf16[4,1,33,6144]{3,2,1,0:T(8,128)(2,1)S(1)} %bitcast.165), channel_id=1, replica_groups=mesh['ctx'=8,'exp'=4] {'exp'}, dimensions={0} | all-to-all | bytes 3244032 | tf_op jit(solution)/shard_map/all_to_all | solution.py:133
  365.7 84.5 %all-gather.8.cloned.1.call-done = bf16[32,1,33,6144]{3,2,1,0:T(8,128)(2,1)} async-done(((bf16[4,1,33,6144]{3,2,1,0:T(8,128)(2,1)}), bf16[32,1,33,6144]{3,2,1,0:T(8,128)(2,1)}) %all-gather.8.cloned.1.call-update) | async-done | bytes 12976144 | tf_op jit(solution)/shard_map/all_gather | solution.py:134
  450.2 25.3 %fusion = f32[32,33,1152]{2,1,0:T(8,128)S(1)} fusion(bf16[32,1,33,6144]{3,2,1,0:T(8,128)(2,1)} %all-gather.8.cloned.1.call-done, bf16[1,6144,1152]{2,1,0:T(8,128)(2,1)} %param.28), kind=kOutput, calls=%fused_computation.2 | convolution fusion | flops 14948499456 | bytes 31997952 | tf_op jit(solution)/shard_map/nemd,edh->nemh/dot_general | solution.py:136
  475.5 27.8 %fusion.19 = bf16[32,33,1152]{2,1,0:T(8,128)(2,1)} fusion(f32[32,33,1152]{2,1,0:T(8,128)S(1)} %fusion, bf16[1,6144,1152]{2,1,0:T(8,128)(2,1)} %param.27, bf16[32,1,33,6144]{3,2,1,0:T(8,128)(2,1)S(1)} %copy-done.10), kind=kOutput, calls=%fused_computation.22 | convolution fusion | flops 14955798528 | bytes 34430976 | tf_op jit(solution)/shard_map/nemd,edh->nemh/dot_general | solution.py:135
  503.3 26.8 %convert_bitcast_fusion = bf16[32,1,33,6144]{3,2,0,1:T(8,128)(2,1)} fusion(bf16[32,33,1152]{2,1,0:T(8,128)(2,1)} %fusion.19, bf16[1,1152,6144]{2,1,0:T(8,128)(2,1)} %param.29), kind=kOutput, calls=%fused_computation.6 | convolution fusion | flops 14954987520 | bytes 29564928 | tf_op jit(solution)/shard_map/nemh,ehd->nemd/dot_general | solution.py:140
  530.1 109.3 %reduce-scatter.5.cloned.1.call-done = bf16[4,1,33,6144]{3,2,0,1:T(8,128)(2,1)} async-done(((bf16[32,1,33,6144]{3,2,0,1:T(8,128)(2,1)}), bf16[4,1,33,6144]{3,2,0,1:T(8,128)(2,1)}) %reduce-scatter.5.cloned.1.call-update) | async-done | bytes 1622032 | tf_op jit(solution)/shard_map/reduce_scatter | solution.py:139
  639.5 4.6 all-to-all-start.1
  644.4 45.0 %all-to-all-done.1 = bf16[4,1,33,6144]{3,2,1,0:T(8,128)(2,1)S(1)} async-done(((bf16[4,1,33,6144]{3,2,1,0:T(8,128)(2,1)}), bf16[4,1,33,6144]{3,2,1,0:T(8,128)(2,1)S(1)}, u32[]{:S(2)}, u32[]{:S(2)}) %all-to-all-start.1) | async-done | bytes 1622048 | tf_op jit(solution)/shard_map/all_to_all | solution.py:147
  689.5 1.7 reshape.179
  691.2 3.8 fusion.10
  (59 shorter events, 3.3 us)
Async XLA Ops:
  6.5 1.2 copy-start
  6.5 100.2 %all-gather.10.cloned.1.call-start = ((), (), s32[]{:S(2)}) async-start(), calls=%async_computation.8 | async-start | bytes 18874368 | tf_op jit(solution)/shard_map/all_gather | solution.py:10
  14.0 0.9 copy-start.11
  14.0 219.4 %all-gather.6.cloned.1.call-start = ((), (), s32[]{:S(2)}) async-start(), calls=%async_computation.4 | async-start | bytes 28311552 | tf_op jit(solution)/shard_map/all_gather | solution.py:106
  14.8 291.9 %reduce-scatter.3.cloned.1.call-start = ((), (), s32[]{:S(2)}) async-start(), calls=%async_computation.5 | async-start | bytes 3932160 | tf_op jit(solution)/shard_map/reduce_scatter | solution.py:108
  109.2 1.2 copy-start.4
  110.4 4.3 copy-start.5
  110.4 4.3 copy-start.7
  246.2 0.7 copy-start.8
  246.2 60.4 %copy-start.2 = (bf16[4,16,6144]{2,1,0:T(8,128)(2,1)S(1)}, bf16[4,16,6144]{2,1,0:T(8,128)(2,1)}, u32[]{:S(2)}) copy-start(bf16[4,16,6144]{2,1,0:T(8,128)(2,1)} %param.23) | copy-start | bytes 2359300
  246.2 62.0 %copy-start.6 = (f32[6144]{0:T(1024)S(1)}, f32[6144]{0:T(1024)}, u32[]{:S(2)}) copy-start(f32[6144]{0:T(1024)} %param.24) | copy-start | bytes 73732
  246.2 203.9 %all-gather.8.cloned.1.call-start = ((), (), s32[]{:S(2)}) async-start(), calls=%async_computation.6 | async-start | bytes 17694720 | tf_op jit(solution)/shard_map/all_gather | solution.py:134
  306.7 1.6 copy-start.3
  365.4 274.0 %reduce-scatter.5.cloned.1.call-start = ((), (), s32[]{:S(2)}) async-start(), calls=%async_computation.7 | async-start | bytes 17694720 | tf_op jit(solution)/shard_map/reduce_scatter | solution.py:139
  450.2 25.3 %copy-start.10 = (bf16[32,1,33,6144]{3,2,1,0:T(8,128)(2,1)S(1)}, bf16[32,1,33,6144]{3,2,1,0:T(8,128)(2,1)}, u32[]{:S(2)}) copy-start(bf16[32,1,33,6144]{3,2,1,0:T(8,128)(2,1)} %all-gather.8.cloned.1.call-done) | copy-start | bytes 38928388
  530.1 114.2 %copy-start.9 = (f32[1,64,2]{1,2,0:T(2,128)S(1)}, f32[1,64,2]{1,2,0:T(2,128)}, u32[]{:S(2)}) copy-start(f32[1,64,2]{1,2,0:T(2,128)} %param.26) | copy-start | bytes 1540
  639.5 50.0 %all-to-all-start.1 = ((bf16[4,1,33,6144]{3,2,1,0:T(8,128)(2,1)}), bf16[4,1,33,6144]{3,2,1,0:T(8,128)(2,1)S(1)}, u32[]{:S(2)}, u32[]{:S(2)}) async-start(bf16[4,1,33,6144]{3,2,1,0:T(8,128)(2,1)} %bitcast.169), calls=%async_computation.3 | async-start | bytes 3932160 | tf_op jit(solution)/shard_map/all_to_all | solution.py:147
  689.5 5.5 copy-start.1
Sparse Core Ops, SparseCore 0:
  14.1 92.5 all-gather.9
  108.6 124.7 all-gather.5
  246.4 60.2 reduce-scatter.2
  365.5 84.5 all-gather.7
  530.2 109.1 reduce-scatter.4
where the time goes:
time: 702 us
  waiting for transfers between devices  486 us (69%)
  matrix products  113 us (16%)
  blocking collectives  64.4 us (9%)
  local copies, waits for them, and re-layouts  14.3 us (2%)
  between operations  14 us (2%)
    all_gather x1, waiting for transfers between devices, body(): full_weight = lax.all_gather(out_weight, 'ctx', axis=1, tiled=True)  117 us
    reduce_scatter x1, waiting for transfers between devices, body(): lax.psum_scatter(jnp.einsum('nemh,ehd->nemd', chosen_rows, w_down, prefer...  109 us
    all_gather x1, waiting for transfers between devices, body(): piece = lax.all_gather(received, 'ctx', axis=0, tiled=True)  84.5 us
    all_gather x1, waiting for transfers between devices, carried_in(): lax.all_gather(a.astype(kind), axis)  71.2 us
    reduce_scatter x1, waiting for transfers between devices, body(): lax.psum_scatter(jnp.dot(chosen_rows, full_weight, preferred_element_type...  59.1 us
    all_to_all x1, blocking collectives, body(): lax.all_to_all(dispatch, 'exp', split_axis=0, concat_axis=0, tiled=True)  49.1 us
    all_to_all x1, waiting for transfers between devices, body(): lax.all_to_all(summed, 'exp', split_axis=0, concat_axis=0, tiled=True)  45 us
    dot_general x1, matrix products, body(): jnp.einsum('nemd,edh->nemh', piece, w_gate, preferred_element_type=jnp.fl...  27.8 us
  transfers between devices with their start and end apart: 6, of which 6 were waited for; matrix products, arithmetic and copies ran while one was open for 2% of the time, Pallas kernels for 0%

commit v1 on v0

v1 whole, which is shorter than its diff:
```python
import functools

import jax
import jax.numpy as jnp
from jax import lax
from jax.experimental import pallas as pl
from jax.experimental.pallas import tpu as pltpu
from jax.sharding import PartitionSpec as P

MIB = 1 << 20
BF = jnp.bfloat16
F32 = jnp.float32


def routes(count):
    bits = [1 << b for b in range(1, count.bit_length() - 1)]
    turn = len(bits) // 2
    return bits, bits[turn:] + bits[:turn]


def hop(count, step):
    both = routes(count)
    return [(i, i ^ both[i & 1][step]) for i in range(count)]


def hop_mask(count, step, side):
    both = routes(count)
    return jnp.where(side == 0, both[0][step], both[1][step])


def pair(count):
    return [(i, i ^ 1) for i in range(count)]


def held_by(count, who):
    held = [who]
    for step in range(len(routes(count)[0])):
        mask = hop_mask(count, step, who & 1)
        held = held + [h ^ mask for h in held]
    return held


def block_order(count, me):
    return held_by(count, me) + held_by(count, me ^ 1)


def send(x, perm):
    return lax.ppermute(x, "ctx", perm)


def joined(parts):
    return parts[0] if len(parts) == 1 else jnp.concatenate(parts, axis=0)


def spread(x, count):
    pieces = [x[None]]
    for step in range(len(routes(count)[0])):
        pieces.append(send(joined(pieces), hop(count, step)))
    pieces.append(send(joined(pieces), pair(count)))
    return pieces


def gathered_sum(near, far, count):
    total = near.astype(F32) + send(far, pair(count)).astype(F32)
    for step in reversed(range(len(routes(count)[0]))):
        half = total.shape[0] // 2
        other = send(total[half:].astype(BF), hop(count, step))
        total = total[:half] + other.astype(F32)
    return total[0]


def sum_over(x, count):
    for bit in range(count.bit_length() - 1):
        x = x + send(x, [(i, i ^ (1 << bit)) for i in range(count)])
    return x


def swap_blocks(x, count, me):
    got = [lax.dynamic_index_in_dim(x, me, 0, False)]
    for j in range(1, count):
        got.append(
            send(
                lax.dynamic_index_in_dim(x, me ^ j, 0, False),
                [(i, i ^ j) for i in range(count)],
            )
        )
    return got


def by_sender(got, count, me):
    stacked = jnp.stack(got)
    return jnp.stack(
        [lax.dynamic_index_in_dim(stacked, me ^ j, 0, False) for j in range(count)]
    )


def state_kernel(dim, k_ref, v_ref, cum_ref, out_ref):
    cum = cum_ref[...]
    fade = jnp.exp(cum[-1:, :] - cum)
    for h in range(cum.shape[1]):
        lanes = slice(h * dim, (h + 1) * dim)
        faded = (k_ref[0, :, lanes].astype(F32) * fade[:, h : h + 1]).astype(BF)
        out_ref[0, h] = lax.dot_general(
            faded, v_ref[0, :, lanes], (((0,), (0,)), ((), ())), preferred_element_type=F32
        ).astype(BF)


def local_states(keys, values, cum, first, seqs):
    _, block, width = keys.shape
    heads = cum.shape[1]
    dim = width // heads
    rows = pl.BlockSpec((1, block, width), lambda s: (s + first, 0, 0))
    return pl.pallas_call(
        functools.partial(state_kernel, dim),
        grid=(seqs,),
        in_specs=[rows, rows, pl.BlockSpec((block, heads), lambda s: (0, 0))],
        out_specs=pl.BlockSpec((1, heads, dim, dim), lambda s: (s, 0, 0, 0)),
        out_shape=jax.ShapeDtypeStruct((seqs, heads, dim, dim), BF),
        compiler_params=pltpu.CompilerParams(vmem_limit_bytes=16 * MIB),
        cost_estimate=pl.CostEstimate(
            flops=2 * seqs * block * width * dim,
            bytes_accessed=4 * seqs * block * width + 2 * seqs * width * dim,
            transcendentals=0,
        ),
    )(keys, values, cum)


def within_kernel(dim, q_ref, k_ref, v_ref, g_ref, cum_ref, cumt_ref, gain_ref, out_ref, act_ref):
    cum = cum_ref[...]
    block = cum.shape[0]
    causal = lax.broadcasted_iota(jnp.int32, (block, block), 0) >= lax.broadcasted_iota(
        jnp.int32, (block, block), 1
    )
    for h in range(cum.shape[1]):
        lanes = slice(h * dim, (h + 1) * dim)
        scores = lax.dot_general(
            q_ref[0, :, lanes],
            k_ref[0, :, lanes],
            (((1,), (1,)), ((), ())),
            preferred_element_type=F32,
        )
        gap = jnp.where(causal, cum[:, h : h + 1] - cumt_ref[h : h + 1, :], -1e30)
        weights = (scores * jnp.exp(gap)).astype(BF)
        out_ref[0, :, lanes] = jnp.dot(weights, v_ref[0, :, lanes], preferred_element_type=F32)
    act_ref[0] = gain_ref[...] * jax.nn.sigmoid(g_ref[0].astype(F32))


def within_block(queries, keys, values, gate, cum, head_gain):
    seqs, block, width = keys.shape
    heads = cum.shape[1]
    dim = width // heads
    rows = pl.BlockSpec((1, block, width), lambda s: (s, 0, 0))
    shape = jax.ShapeDtypeStruct((seqs, block, width), F32)
    return pl.pallas_call(
        functools.partial(within_kernel, dim),
        grid=(seqs,),
        in_specs=[
            rows,
            rows,
            rows,
            rows,
            pl.BlockSpec((block, heads), lambda s: (0, 0)),
            pl.BlockSpec((heads, block), lambda s: (0, 0)),
            pl.BlockSpec((1, width), lambda s: (0, 0)),
        ],
        out_specs=[rows, rows],
        out_shape=[shape, shape],
        compiler_params=pltpu.CompilerParams(vmem_limit_bytes=24 * MIB),
        cost_estimate=pl.CostEstimate(
            flops=4 * seqs * block * block * width,
            bytes_accessed=16 * seqs * block * width,
            transcendentals=seqs * block * width,
        ),
    )(queries, keys, values, gate, cum, cum.T, head_gain[None])


def mixed_kernel(dim, sub, q_ref, state_ref, within_ref, act_ref, cum_ref, out_ref):
    scale = jnp.exp(cum_ref[...])
    for h in range(scale.shape[1]):
        lanes = slice(h * dim, (h + 1) * dim)
        carried = jnp.dot(q_ref[0, :, lanes], state_ref[0, h], preferred_element_type=F32)
        attended = within_ref[0, :, lanes] + carried * scale[:, h : h + 1]
        square = jnp.mean(attended * attended, axis=1, keepdims=True)
        mixed = (attended * lax.rsqrt(square + 1e-06) * act_ref[0, :, lanes]).astype(BF)
        for d in range(out_ref.shape[0]):
            out_ref[d, 0, :, lanes] = mixed[d * sub : (d + 1) * sub]


def mixed_rows(queries, states, within, act, cum, first, sub):
    seqs, heads, dim, _ = states.shape
    block, width = queries.shape[1:]
    parts = block // sub
    rows = pl.BlockSpec((1, block, width), lambda s: (s + first, 0, 0))
    return pl.pallas_call(
        functools.partial(mixed_kernel, dim, sub),
        grid=(seqs,),
        in_specs=[
            rows,
            pl.BlockSpec((1, heads, dim, dim), lambda s: (s, 0, 0, 0)),
            rows,
            rows,
            pl.BlockSpec((block, heads), lambda s: (0, 0)),
        ],
        out_specs=pl.BlockSpec((parts, 1, sub, width), lambda s: (0, s, 0, 0)),
        out_shape=jax.ShapeDtypeStruct((parts, seqs, sub, width), BF),
        compiler_params=pltpu.CompilerParams(vmem_limit_bytes=16 * MIB),
        cost_estimate=pl.CostEstimate(
            flops=2 * seqs * block * width * dim,
            bytes_accessed=12 * seqs * block * width + 2 * seqs * width * dim,
            transcendentals=0,
        ),
    )(queries, states, within, act, cum)


def project_kernel(sizes, order_ref, *refs):
    pieces, w_ref, out_ref = refs[:-2], refs[-2], refs[-1]
    parts, _, rows, _ = out_ref.shape
    at = 0
    for ref, size in zip(pieces, sizes):
        for i in range(size):
            product = jnp.dot(ref[i], w_ref[...], preferred_element_type=F32).astype(BF)
            for d in range(parts):
                out_ref[d, order_ref[at]] = product[d * rows : (d + 1) * rows]
            at += 1


def project(pieces, weight, order, parts):
    count = sum(p.shape[0] for p in pieces)
    rows, depth = pieces[0].shape[1:]
    cols = weight.shape[1]
    whole = pl.BlockSpec(memory_space=pltpu.VMEM)
    return pl.pallas_call(
        functools.partial(project_kernel, [p.shape[0] for p in pieces]),
        in_specs=[pl.BlockSpec(memory_space=pltpu.SMEM)] + [whole] * (len(pieces) + 1),
        out_specs=whole,
        out_shape=jax.ShapeDtypeStruct((parts, count, rows // parts, cols), BF),
        compiler_params=pltpu.CompilerParams(vmem_limit_bytes=20 * MIB),
        cost_estimate=pl.CostEstimate(
            flops=2 * count * rows * depth * cols,
            bytes_accessed=2 * (count * rows * (depth + cols) + depth * cols),
            transcendentals=0,
        ),
    )(order, *pieces, weight)


def expert_kernel(sizes, order_ref, *refs):
    count = sum(sizes)
    half = count // 2
    pieces = refs[: len(sizes)]
    scale_ref, gate_ref, up_ref, down_ref, near_ref, far_ref, g_acc, u_acc, hidden = refs[
        len(sizes) :
    ]
    i = pl.program_id(0)

    @pl.when(i == 0)
    def _():
        g_acc[...] = jnp.dot(pieces[0][0], gate_ref[...], preferred_element_type=F32)
        u_acc[...] = jnp.dot(pieces[0][0], up_ref[...], preferred_element_type=F32)

    start = 0
    for ref, size in zip(pieces, sizes):
        if start > 0:

            @pl.when((i >= start) & (i < start + size))
            def _(ref=ref):
                g_acc[...] += jnp.dot(ref[0], gate_ref[...], preferred_element_type=F32)
                u_acc[...] += jnp.dot(ref[0], up_ref[...], preferred_element_type=F32)

        start += size

    @pl.when(i == count - 1)
    def _():
        scale = scale_ref[...]
        g = g_acc[...] * scale
        hidden[...] = (g / (1.0 + jnp.exp(-g)) * (u_acc[...] * scale)).astype(BF)

    @pl.when((i >= count) & (i < count + half))
    def _():
        far_ref[0] = jnp.dot(hidden[...], down_ref[...], preferred_element_type=F32).astype(BF)

    @pl.when(i >= count + half)
    def _():
        near_ref[0] = jnp.dot(hidden[...], down_ref[...], preferred_element_type=F32).astype(BF)


def expert(pieces, scale, w_gate, w_up, w_down, order):
    sizes = [p.shape[0] for p in pieces]
    count = sum(sizes)
    half = count // 2
    rows, cols = pieces[0].shape[1:]
    depth, hid = w_gate.shape

    def up_map(i, order):
        return (order[jnp.minimum(i, count - 1)], 0)

    def down_map(i, order):
        j = jnp.maximum(i - count, 0)
        return (0, order[jnp.where(j < half, j + half, j - half)])

    specs = []
    start = 0
    for size in sizes:
        specs.append(
            pl.BlockSpec(
                (1, rows, cols),
                lambda i, order, start=start, size=size: (
                    jnp.clip(i - start, 0, size - 1),
                    0,
                    0,
                ),
            )
        )
        start += size
    out = jax.ShapeDtypeStruct((half, rows, cols), BF)
    return pl.pallas_call(
        functools.partial(expert_kernel, sizes),
        grid_spec=pltpu.PrefetchScalarGridSpec(
            num_scalar_prefetch=1,
            grid=(2 * count,),
            in_specs=specs
            + [
                pl.BlockSpec((rows, 1), lambda i, order: (0, 0)),
                pl.BlockSpec((cols, hid), up_map),
                pl.BlockSpec((cols, hid), up_map),
                pl.BlockSpec((hid, cols), down_map),
            ],
            out_specs=[
                pl.BlockSpec(
                    (1, rows, cols),
                    lambda i, order: (jnp.clip(i - count - half, 0, half - 1), 0, 0),
                ),
                pl.BlockSpec(
                    (1, rows, cols), lambda i, order: (jnp.clip(i - count, 0, half - 1), 0, 0)
                ),
            ],
            scratch_shapes=[
                pltpu.VMEM((rows, hid), F32),
                pltpu.VMEM((rows, hid), F32),
                pltpu.VMEM((rows, hid), BF),
            ],
        ),
        out_shape=[out, out],
        compiler_params=pltpu.CompilerParams(vmem_limit_bytes=32 * MIB),
        cost_estimate=pl.CostEstimate(
            flops=6 * rows * depth * hid,
            bytes_accessed=6 * depth * hid + 4 * rows * depth,
            transcendentals=rows * hid,
        ),
    )(order, *pieces, scale, w_gate, w_up, w_down)


def body(
    queries,
    keys,
    values,
    decay_log,
    out_gate,
    head_gain,
    out_weight,
    stream,
    norm_gain,
    expert_ids,
    expert_share,
    w_gate,
    w_up,
    w_down,
):
    count = lax.axis_size("ctx")
    parts = lax.axis_size("exp")
    me = lax.axis_index("ctx")
    mine = lax.axis_index("exp")
    side = me & 1
    seqs, block, width = queries.shape
    heads = decay_log.shape[1]
    sub, model = stream.shape[1:]
    tokens = seqs * sub
    cols = model // count
    order = block_order(count, me)
    order_array = jnp.stack(order).astype(jnp.int32)

    cum = jnp.cumsum(decay_log, axis=0)
    small = jnp.concatenate(
        [
            expert_ids.reshape(2 * tokens).astype(F32),
            expert_share.reshape(2 * tokens),
            cum[-1],
        ]
    )
    width_small = small.shape[0]
    small = jnp.pad(small, (0, -width_small % 128)).reshape(-1, 128)
    facts = joined(spread(small, count)).reshape(count, -1)
    place = order_array[None, :] == jnp.arange(count, dtype=jnp.int32)[:, None]
    facts = jnp.sum(jnp.where(place[:, :, None], facts[None], 0.0), axis=1)
    ids = facts[:, : 2 * tokens].astype(jnp.int32)
    shares = facts[:, 2 * tokens : 4 * tokens]
    ends = facts[:, 4 * tokens : 4 * tokens + heads]

    stream_cols = stream.reshape(tokens, count, cols).transpose(1, 0, 2)
    stream_got = swap_blocks(stream_cols, count, me)

    block_no = jnp.arange(count)

    def faded(source, target):
        between = (block_no >= 2 * (source // 2 + 1)) & (block_no < 2 * (target // 2))
        power = jnp.sum(jnp.where(between[:, None], ends, 0.0), axis=0)
        return jnp.where(source // 2 < target // 2, jnp.exp(power), 0.0)

    def at_heads(row):
        return row[None, :, None, None]

    half_heads = heads // 2

    def side_half(x, axis):
        return lax.dynamic_slice_in_dim(x, side * half_heads, half_heads, axis)

    fade_own = jnp.exp(lax.dynamic_index_in_dim(ends, me, 0, False))
    fade_other = jnp.exp(lax.dynamic_index_in_dim(ends, me ^ 1, 0, False))
    steps = len(routes(count)[0])

    def arriving(own, other):
        fade_late = jnp.where(side == 0, fade_other, fade_own)
        own_half, other_half = side_half(own, 1).astype(F32), side_half(other, 1).astype(F32)
        early = jnp.where(side == 0, own_half, other_half)
        late = jnp.where(side == 0, other_half, own_half)
        chip = (at_heads(side_half(fade_late, 0)) * early + late).astype(BF)
        held, names = [chip], [me]
        for step in range(steps - 1):
            stacked = jnp.stack(held)
            got = send(stacked, hop(count, step))
            mask = hop_mask(count, step, side)
            held = held + [got[i] for i in range(len(held))]
            names = names + [name ^ mask for name in names]

        def towards(target):
            return sum(
                at_heads(side_half(faded(name, target), 0)) * state.astype(F32)
                for name, state in zip(names, held)
            )

        entering = towards(me)
        if steps:
            there = me ^ hop_mask(count, steps - 1, side)
            entering = entering + send(towards(there).astype(BF), hop(count, steps - 1)).astype(F32)
        entering = entering.astype(BF)
        entering_other = send(entering, pair(count))
        low = jnp.where(side == 0, entering, entering_other)
        high = jnp.where(side == 0, entering_other, entering)
        entering = jnp.concatenate([low, high], axis=1).astype(F32)
        second = at_heads(fade_other) * entering + other.astype(F32)
        return jnp.where(side == 0, entering, second).astype(BF)

    halves = 2
    each = seqs // halves
    own_states = [local_states(keys, values, cum, h * each, each) for h in range(halves)]
    other_states = [send(own, pair(count)) for own in own_states]
    within, act = within_block(queries, keys, values, out_gate, cum, head_gain)
    projected = []
    for h in range(halves):
        states = arriving(own_states[h], other_states[h])
        mixed = mixed_rows(queries, states, within, act, cum, h * each, sub)
        pieces = spread(mixed.reshape(parts * each * sub, width), count)
        partial = project(pieces, out_weight, order_array, parts)

        def part(index):
            return lax.dynamic_index_in_dim(
                partial, jnp.clip(index, 0, parts - 1), 0, False
            ).astype(F32)

        total = part(mine)
        for way in (1, -1):
            passed = None
            for t in range(parts - 1):
                if way == 1:
                    perm = [(i, i + 1) for i in range(parts - 1) if i <= t]
                else:
                    perm = [(i, i - 1) for i in range(1, parts) if parts - 1 - i <= t]
                running = part(mine + way * (parts - 1 - t))
                if passed is not None:
                    running = running + passed.astype(F32)
                passed = lax.ppermute(running.astype(BF), "exp", perm)
            if passed is not None:
                total = total + passed.astype(F32)
        projected.append(total)
    stream_all = by_sender(stream_got, count, me)
    residual = stream_all.astype(F32) + jnp.concatenate(projected, axis=1)
    residual = residual.reshape(count * tokens, cols)

    square = sum_over(jnp.sum(residual * residual, axis=1), count)
    scale = lax.rsqrt(square / model + 1e-06)
    gain = lax.dynamic_slice_in_dim(norm_gain, me * cols, cols, 0)
    rows_in = (residual * gain).astype(BF)

    expert_local = w_gate.shape[0]
    experts = expert_local * parts
    capacity = max(2, (2 * tokens + experts - 1) // experts + 1)
    one_hot = ids[:, :, None] == jnp.arange(experts, dtype=jnp.int32)
    earlier = jnp.arange(2 * tokens)[:, None] > jnp.arange(2 * tokens)[None, :]
    ahead = jnp.einsum(
        "tu,gue->gte", earlier.astype(BF), one_hot.astype(BF), preferred_element_type=F32
    )
    ranking = jnp.sum(jnp.where(one_hot, ahead, 0.0), axis=2).astype(jnp.int32)
    slots = capacity * count
    turned = (ids - mine + experts) % experts
    slot_of = (turned * count + jnp.arange(count, dtype=jnp.int32)[:, None]) * capacity + ranking
    slot_of = slot_of.reshape(count * tokens, 2)
    share_of = shares.reshape(count * tokens, 2)
    returned = []
    for turn in range(parts):
        numbers = turn * slots + jnp.arange(slots, dtype=jnp.int32)
        hit = [slot_of[:, k][None, :] == numbers[:, None] for k in range(2)]
        placing = hit[0] | hit[1]
        dispatch = jnp.dot(placing.astype(BF), rows_in, preferred_element_type=F32).astype(BF)
        slot_scale = jnp.sum(jnp.where(placing, scale[None, :], 0.0), axis=1)
        forth = [(i, (i + turn) % parts) for i in range(parts)]
        back = [(j, i) for i, j in forth]
        if turn:
            dispatch = lax.ppermute(dispatch, "exp", forth)
            slot_scale = lax.ppermute(slot_scale, "exp", forth)
        pieces = spread(dispatch, count)
        near, far = expert(
            pieces, slot_scale[:, None], w_gate[0], w_up[0], w_down[0], order_array
        )
        done = gathered_sum(near, far, count).astype(BF)
        if turn:
            done = lax.ppermute(done, "exp", back)
        returned.append(done)
    result = residual
    for turn in range(parts):
        numbers = turn * slots + jnp.arange(slots, dtype=jnp.int32)
        weighting = sum(
            jnp.where(slot_of[:, k][:, None] == numbers[None, :], share_of[:, k][:, None], 0.0)
            for k in range(2)
        )
        high = weighting.astype(BF)
        low = (weighting - high.astype(F32)).astype(BF)
        result = result + jnp.dot(high, returned[turn], preferred_element_type=F32)
        result = result + jnp.dot(low, returned[turn], preferred_element_type=F32)
    result = result.astype(BF).reshape(count, tokens, cols)
    result = by_sender(swap_blocks(result, count, me), count, me)
    return result.transpose(1, 0, 2).reshape(seqs, sub, model)


def solution(mesh):
    return jax.shard_map(
        body,
        mesh=mesh,
        in_specs=(
            P(None, "ctx", "exp"),
            P(None, "ctx", "exp"),
            P(None, "ctx", "exp"),
            P("ctx", "exp"),
            P(None, "ctx", "exp"),
            P("exp"),
            P("exp", "ctx"),
            P(None, ("ctx", "exp"), None),
            P(),
            P(("ctx", "exp"), None, None),
            P(("ctx", "exp"), None, None),
            P("exp", None, "ctx"),
            P("exp", None, "ctx"),
            P("exp", "ctx", None),
        ),
        out_specs=P(None, ("ctx", "exp"), None),
        check_vma=False,
    )
```

time: 702 us -> 540 us (0.77); the launches traced: 702 us -> 530 us
  waiting for transfers between devices: 486 us -> 193 us
  Pallas kernels: 0 us -> 126 us
  starting transfers between devices: 4.99 us -> 113 us
  matrix products: 113 us -> 8.45 us
  blocking collectives: 64.4 us -> 0 us
  other arithmetic: 4.44 us -> 39.2 us
  local copies, waits for them, and re-layouts: 14.3 us -> 47.9 us
  between operations: 14 us -> 1.71 us
    all_gather x3 -> x0, waiting for transfers between devices: 272 us -> none  [the longest x1 117 us: body(): full_weight = lax.all_gather(out_weight, 'ctx', axis=1, tiled=True)]
    ppermute x0 -> x79, waiting for transfers between devices: none -> 193 us  [the longest x58 119 us: send(): return lax.ppermute(x, 'ctx', perm)]
    reduce_scatter x2 -> x0, waiting for transfers between devices: 168 us -> none  [the longest x1 109 us: body(): lax.psum_scatter(jnp.einsum('nemh,ehd->nemd', chosen_rows, w_down, prefer...]
    pallas_call x0 -> x11, Pallas kernels: none -> 126 us  [the longest x4 98 us: expert(): pl.pallas_call(functools.partial(expert_kernel, sizes), grid_spec=pltpu.P...]
    ppermute x0 -> x79, starting transfers between devices: none -> 113 us  [the longest x58 60 us: send(): return lax.ppermute(x, 'ctx', perm)]
    dot_general x9 -> x13, matrix products: 113 us -> 8.45 us  [the longest x4 3.63 us: body(): result = result + jnp.dot(low, returned[turn], preferred_element_type=F32)]
    all_to_all x1 -> x0, blocking collectives: 49.1 us -> none  [body(): lax.all_to_all(dispatch, 'exp', split_axis=0, concat_axis=0, tiled=True)]
    all_to_all x1 -> x0, waiting for transfers between devices: 45 us -> none  [body(): lax.all_to_all(summed, 'exp', split_axis=0, concat_axis=0, tiled=True)]
  transfers between devices with their start and end apart: 6 -> 79, of which waited for: 6 -> 40; matrix products, arithmetic and copies ran while one was open for 2% -> 9% of each run, Pallas kernels for 0% -> 23%
where the time goes in v1:
time: 540 us; the launch traced here: 530 us
  waiting for transfers between devices  193 us (36%)
  Pallas kernels  126 us (23%)
  starting transfers between devices  113 us (21%)
  local copies, waits for them, and re-layouts  47.9 us (9%)
  other arithmetic  39.2 us (7%)
  matrix products  8.45 us (2%)
    ppermute x58, waiting for transfers between devices, send(): return lax.ppermute(x, 'ctx', perm)  119 us
    pallas_call x4, Pallas kernels, expert(): pl.pallas_call(functools.partial(expert_kernel, sizes), grid_spec=pltpu.P...  98 us
    ppermute x58, starting transfers between devices, send(): return lax.ppermute(x, 'ctx', perm)  60 us
    unnamed x109, local copies, waits for them, and re-layouts  39.9 us
    ppermute x12, waiting for transfers between devices, body(): passed = lax.ppermute(running.astype(BF), 'exp', perm)  32.6 us
    ppermute x12, starting transfers between devices, body(): passed = lax.ppermute(running.astype(BF), 'exp', perm)  28.9 us
    ppermute x3, waiting for transfers between devices, body(): done = lax.ppermute(done, 'exp', back)  24.9 us
    ppermute x3, starting transfers between devices, body(): dispatch = lax.ppermute(dispatch, 'exp', forth)  20.7 us
  transfers between devices with their start and end apart: 79, of which 40 were waited for; matrix products, arithmetic and copies ran while one was open for 9% of the time, Pallas kernels for 23%

profile of v1, /device:TPU:0, one launch (start us, length us, event | category | flops | bytes accessed | tf_op | source)
XLA Modules:
  0.0 529.7 jit_solution(8089331296015252463)
XLA Ops:
  21.0 7.2 %collective-permute-done.11 = bf16[1,2,8,128,128]{4,3,2,1,0:T(8,128)(2,1)S(1)} collective-permute-done((bf16[1,2,8,128,128]{4,3,2,1,0:T(8,128)(2,1)}, bf16[1,2,8,128,128]{4,3,2,1,0:T(8,128)(2,1)S(1)}, u32[]{:S(2)}, u32[]{:S(2)}) %collective-permute-start.11) | collective-permute-done | bytes 524320 | tf_op jit(solution)/shard_map/ppermute | solution.py:48
  28.2 5.6 %collective-permute-done.24 = bf16[1,2,8,128,128]{4,3,2,1,0:T(8,128)(2,1)S(1)} collective-permute-done((bf16[1,2,8,128,128]{4,3,2,1,0:T(8,128)(2,1)}, bf16[1,2,8,128,128]{4,3,2,1,0:T(8,128)(2,1)S(1)}, u32[]{:S(2)}, u32[]{:S(2)}) %collective-permute-start.24) | collective-permute-done | bytes 524320 | tf_op jit(solution)/shard_map/ppermute | solution.py:48
  38.9 7.4 %collective-permute-done.12 = bf16[2,8,128,128]{3,2,1,0:T(8,128)(2,1)} collective-permute-done((bf16[2,8,128,128]{3,2,1,0:T(8,128)(2,1)}, bf16[2,8,128,128]{3,2,1,0:T(8,128)(2,1)}, u32[]{:S(2)}, u32[]{:S(2)}) %collective-permute-start.12) | collective-permute-done | bytes 524320 | tf_op jit(solution)/shard_map/ppermute | solution.py:48
  46.3 5.6 %collective-permute-done.25 = bf16[2,8,128,128]{3,2,1,0:T(8,128)(2,1)} collective-permute-done((bf16[2,8,128,128]{3,2,1,0:T(8,128)(2,1)}, bf16[2,8,128,128]{3,2,1,0:T(8,128)(2,1)}, u32[]{:S(2)}, u32[]{:S(2)}) %collective-permute-start.25) | collective-permute-done | bytes 524320 | tf_op jit(solution)/shard_map/ppermute | solution.py:48
  57.3 9.1 %shard_map.137 = (f32[4,64,2048]{2,1,0:T(8,128)S(1)}, f32[4,64,2048]{2,1,0:T(8,128)S(1)}) custom-call(bf16[4,64,2048]{2,1,0:T(8,128)(2,1)S(1)} %copy-done.7, bf16[4,64,2048]{2,1,0:T(8,128)(2,1)S(1)} %copy-done.4, bf16[4,64,2048]{2,1,0:T(8,128)(2,1)S(1)} %copy-done.6, bf16[4,64,2048]{2,1,0:T(8,128)(2,1)S(1)} %copy-done.20, ...), custom_call_target="tpu_custom_call" | custom-call | flops 134217728 | bytes 8388608 | tf_op jit(solution)/shard_map/pallas_call | solution.py:154
  107.2 10.6 %collective-permute-done.15.refs_2_ = bf16[2,128,2048]{2,1,0:T(8,128)(2,1)} collective-permute-done((bf16[2,128,2048]{2,1,0:T(8,128)(2,1)}, bf16[2,128,2048]{2,1,0:T(8,128)(2,1)}, u32[]{:S(2)}, u32[]{:S(2)}) %collective-permute-start.15) | collective-permute-done | bytes 1048608 | tf_op jit(solution)/shard_map/ppermute | solution.py:48
  131.5 5.3 %shard_map.142 = bf16[4,8,32,768]{3,2,1,0:T(8,128)(2,1)S(1)} custom-call(s32[8]{0:T(128)S(1)} %stack.122.order_ref, bf16[1,128,2048]{2,1,0:T(8,128)(2,1)S(1)} %bitcast.215, bf16[1,128,2048]{2,1,0:T(8,128)(2,1)S(1)} %copy-done.11, bf16[2,128,2048]{2,1,0:T(8,128)(2,1)S(1)} %collective-permute-done.28.refs_2_, ...), custom_call_target="tpu_custom_call" | custom-call | flops 3221225472 | bytes 8912896 | tf_op jit(solution)/shard_map/pallas_call | solution.py:232
  140.4 4.9 shard_map.139
  149.9 4.4 collective-permute-start.31
  158.4 4.8 collective-permute-start.18
  167.6 6.7 %collective-permute-done.18 = bf16[8,32,768]{2,1,0:T(8,128)(2,1)S(1)} collective-permute-done((bf16[8,32,768]{2,1,0:T(8,128)(2,1)S(1)}, bf16[8,32,768]{2,1,0:T(8,128)(2,1)S(1)}, u32[]{:S(2)}, u32[]{:S(2)}) %collective-permute-start.18) | collective-permute-done | bytes 393248 | tf_op jit(solution)/shard_map/ppermute | solution.py:480
  175.2 5.0 collective-permute-start.32
  180.3 4.6 collective-permute-start.19
  189.8 9.1 %collective-permute-done.35 = bf16[8,32,768]{2,1,0:T(8,128)(2,1)S(1)} collective-permute-done((bf16[8,32,768]{2,1,0:T(8,128)(2,1)S(1)}, bf16[8,32,768]{2,1,0:T(8,128)(2,1)S(1)}, u32[]{:S(2)}, u32[]{:S(2)}) %collective-permute-start.35) | collective-permute-done | bytes 393248 | tf_op jit(solution)/shard_map/ppermute | solution.py:480
  199.0 5.7 %collective-permute-done.22 = bf16[8,32,768]{2,1,0:T(8,128)(2,1)S(1)} collective-permute-done((bf16[8,32,768]{2,1,0:T(8,128)(2,1)S(1)}, bf16[8,32,768]{2,1,0:T(8,128)(2,1)S(1)}, u32[]{:S(2)}, u32[]{:S(2)}) %collective-permute-start.22) | collective-permute-done | bytes 393248 | tf_op jit(solution)/shard_map/ppermute | solution.py:480
  208.0 6.7 %collective-permute-done.36.refs_1_ = bf16[1,264,768]{2,1,0:T(8,128)(2,1)S(1)} collective-permute-done((bf16[1,264,768]{2,1,0:T(8,128)(2,1)S(1)}, bf16[1,264,768]{2,1,0:T(8,128)(2,1)S(1)}, u32[]{:S(2)}, u32[]{:S(2)}) %collective-permute-start.36) | collective-permute-done | bytes 405536 | tf_op jit(solution)/shard_map/ppermute | solution.py:48
  219.7 20.6 %collective-permute-start.45 = (bf16[264,768]{1,0:T(8,128)(2,1)S(1)}, bf16[264,768]{1,0:T(8,128)(2,1)S(1)}, u32[]{:S(2)}, u32[]{:S(2)}) collective-permute-start(bf16[264,768]{1,0:T(8,128)(2,1)S(1)} %convolution_convert_fusion.2), channel_id=1, source_target_pairs={{0,1},{1,2},{2,3},{3,0},{4,5},{5,6},{6,7},{7,4},{8,9},{9,10},{10,1... | collective-permute-start | bytes 1216520 | tf_op jit(solution)/shard_map/ppermute | solution.py:517
  250.0 6.5 %collective-permute-done.55.refs_1_ = bf16[1,264,768]{2,1,0:T(8,128)(2,1)S(1)} collective-permute-done((bf16[1,264,768]{2,1,0:T(8,128)(2,1)S(1)}, bf16[1,264,768]{2,1,0:T(8,128)(2,1)S(1)}, u32[]{:S(2)}, u32[]{:S(2)}) %collective-permute-start.55) | collective-permute-done | bytes 405536 | tf_op jit(solution)/shard_map/ppermute | solution.py:48
  258.6 6.6 %collective-permute-done.46.refs_1_ = bf16[1,264,768]{2,1,0:T(8,128)(2,1)S(1)} collective-permute-done((bf16[1,264,768]{2,1,0:T(8,128)(2,1)S(1)}, bf16[1,264,768]{2,1,0:T(8,128)(2,1)S(1)}, u32[]{:S(2)}, u32[]{:S(2)}) %collective-permute-start.46) | collective-permute-done | bytes 405536 | tf_op jit(solution)/shard_map/ppermute | solution.py:48
  274.5 9.8 %collective-permute-start.66 = (bf16[4,264,768]{2,1,0:T(8,128)(2,1)S(1)}, bf16[4,264,768]{2,1,0:T(8,128)(2,1)S(1)}, u32[]{:S(2)}, u32[]{:S(2)}) collective-permute-start(bf16[4,264,768]{2,1,0:T(8,128)(2,1)S(1)} %pad_maximum_fusion.5), channel_id=1, source_target_pairs={{0,4},{4,0},{8,12},{12,8},{16,20},{20,16},{24,28},{28,24},{1,5},{5... | collective-permute-start | bytes 4866056 | tf_op jit(solution)/shard_map/ppermute | solution.py:48
  302.8 5.0 copy-done
  307.9 24.5 %shard_map.143 = (bf16[4,264,768]{2,1,0:T(8,128)(2,1)S(1)}, bf16[4,264,768]{2,1,0:T(8,128)(2,1)}) custom-call(s32[8]{0:T(128)S(1)} %stack.122.order_ref, bf16[1,264,768]{2,1,0:T(8,128)(2,1)S(1)} %fusion.13.refs_0_, bf16[1,264,768]{2,1,0:T(8,128)(2,1)S(1)} %collective-permute-done.36.refs_1_, bf16[2,264,768]{2,1,0:T(8,128)(2,1)S(1)} %copy-done.9, ...), custom_call_target="tpu_custom_call" | custom-call | flops 11211374592 | bytes 48955392 | tf_op jit(solution)/shard_map/pallas_call | solution.py:315
  333.6 5.0 copy-done.1
  338.6 24.4 %shard_map.146 = (bf16[4,264,768]{2,1,0:T(8,128)(2,1)S(1)}, bf16[4,264,768]{2,1,0:T(8,128)(2,1)}) custom-call(s32[8]{0:T(128)S(1)} %stack.122.order_ref, bf16[1,264,768]{2,1,0:T(8,128)(2,1)S(1)} %bitcast.223, bf16[1,264,768]{2,1,0:T(8,128)(2,1)S(1)} %collective-permute-done.64.refs_1_, bf16[2,264,768]{2,1,0:T(8,128)(2,1)} %collective-permute-done.65.refs_2_, ...), custom_call_target="tpu_custom_call" | custom-call | flops 11211374592 | bytes 48955392 | tf_op jit(solution)/shard_map/pallas_call | solution.py:315
  364.6 5.0 copy-done.2
  369.6 24.6 %shard_map.145 = (bf16[4,264,768]{2,1,0:T(8,128)(2,1)S(1)}, bf16[4,264,768]{2,1,0:T(8,128)(2,1)}) custom-call(s32[8]{0:T(128)S(1)} %stack.122.order_ref, bf16[1,264,768]{2,1,0:T(8,128)(2,1)S(1)} %bitcast.227, bf16[1,264,768]{2,1,0:T(8,128)(2,1)S(1)} %collective-permute-done.55.refs_1_, bf16[2,264,768]{2,1,0:T(8,128)(2,1)} %collective-permute-done.56.refs_2_, ...), custom_call_target="tpu_custom_call" | custom-call | flops 11211374592 | bytes 48955392 | tf_op jit(solution)/shard_map/pallas_call | solution.py:315
  395.5 24.6 %shard_map.144 = (bf16[4,264,768]{2,1,0:T(8,128)(2,1)S(1)}, bf16[4,264,768]{2,1,0:T(8,128)(2,1)}) custom-call(s32[8]{0:T(128)S(1)} %stack.122.order_ref, bf16[1,264,768]{2,1,0:T(8,128)(2,1)S(1)} %bitcast.219, bf16[1,264,768]{2,1,0:T(8,128)(2,1)S(1)} %collective-permute-done.46.refs_1_, bf16[2,264,768]{2,1,0:T(8,128)(2,1)} %collective-permute-done.47.refs_2_, ...), custom_call_target="tpu_custom_call" | custom-call | flops 11211374592 | bytes 48955392 | tf_op jit(solution)/shard_map/pallas_call | solution.py:315
  438.5 10.9 %collective-permute-done.69 = bf16[2,264,768]{2,1,0:T(8,128)(2,1)S(1)} collective-permute-done((bf16[2,264,768]{2,1,0:T(8,128)(2,1)S(1)}, bf16[2,264,768]{2,1,0:T(8,128)(2,1)S(1)}, u32[]{:S(2)}, u32[]{:S(2)}) %collective-permute-start.69) | collective-permute-done | bytes 811040 | tf_op jit(solution)/shard_map/ppermute | solution.py:48
  451.5 11.0 %collective-permute-done.60 = bf16[2,264,768]{2,1,0:T(8,128)(2,1)S(1)} collective-permute-done((bf16[2,264,768]{2,1,0:T(8,128)(2,1)S(1)}, bf16[2,264,768]{2,1,0:T(8,128)(2,1)S(1)}, u32[]{:S(2)}, u32[]{:S(2)}) %collective-permute-start.60) | collective-permute-done | bytes 811040 | tf_op jit(solution)/shard_map/ppermute | solution.py:48
  464.6 10.9 %collective-permute-done.51 = bf16[2,264,768]{2,1,0:T(8,128)(2,1)S(1)} collective-permute-done((bf16[2,264,768]{2,1,0:T(8,128)(2,1)S(1)}, bf16[2,264,768]{2,1,0:T(8,128)(2,1)S(1)}, u32[]{:S(2)}, u32[]{:S(2)}) %collective-permute-start.51) | collective-permute-done | bytes 811040 | tf_op jit(solution)/shard_map/ppermute | solution.py:48
  483.9 21.7 %collective-permute-done.62 = bf16[264,768]{1,0:T(8,128)(2,1)S(1)} collective-permute-done((bf16[264,768]{1,0:T(8,128)(2,1)S(1)}, bf16[264,768]{1,0:T(8,128)(2,1)S(1)}, u32[]{:S(2)}, u32[]{:S(2)}) %collective-permute-start.62) | collective-permute-done | bytes 405536 | tf_op jit(solution)/shard_map/ppermute | solution.py:525
  522.2 5.1 collective-permute-done.76
  (361 shorter events, 209.2 us)
Async XLA Ops:
  78.7 22.9 %collective-permute-start.14 = (bf16[1,128,2048]{2,1,0:T(8,128)(2,1)S(1)}, bf16[1,128,2048]{2,1,0:T(8,128)(2,1)S(1)}, u32[]{:S(2)}, u32[]{:S(2)}) collective-permute-start(bf16[1,128,2048]{2,1,0:T(8,128)(2,1)S(1)} %bitcast.208), channel_id=1, source_target_pairs={{0,8},{4,20},{8,0},{12,28},{16,24},{20,4},{24,16},{28,12},{1,9},{5... | collective-permute-start | bytes 1572872 | tf_op jit(solution)/shard_map/ppermute | solution.py:48
  85.5 19.3 %collective-permute-start.28 = (bf16[2,128,2048]{2,1,0:T(8,128)(2,1)}, bf16[2,128,2048]{2,1,0:T(8,128)(2,1)S(1)}, u32[]{:S(2)}, u32[]{:S(2)}) collective-permute-start(bf16[2,128,2048]{2,1,0:T(8,128)(2,1)} %pad_maximum_fusion.7), channel_id=1, source_target_pairs={{0,16},{4,12},{8,24},{12,4},{16,0},{20,28},{24,8},{28,20},{1,17},{... | collective-permute-start | bytes 3145736 | tf_op jit(solution)/shard_map/ppermute | solution.py:48
  91.2 28.5 %collective-permute-start = (bf16[64,768]{1,0:T(8,128)(2,1)}, bf16[64,768]{1,0:T(8,128)(2,1)}, u32[]{:S(2)}, u32[]{:S(2)}) collective-permute-start(bf16[64,768]{1,0:T(8,128)(2,1)} %bitcast.203), channel_id=1, source_target_pairs={{0,4},{4,0},{8,12},{12,8},{16,20},{20,16},{24,28},{28,24},{1,5},{5... | collective-permute-start | bytes 294920 | tf_op jit(solution)/shard_map/ppermute | solution.py:48
  91.9 29.6 %collective-permute-start.1 = (bf16[64,768]{1,0:T(8,128)(2,1)}, bf16[64,768]{1,0:T(8,128)(2,1)}, u32[]{:S(2)}, u32[]{:S(2)}) collective-permute-start(bf16[64,768]{1,0:T(8,128)(2,1)} %bitcast.202), channel_id=1, source_target_pairs={{0,8},{4,12},{8,0},{12,4},{16,24},{20,28},{24,16},{28,20},{1,9},{5... | collective-permute-start | bytes 294920 | tf_op jit(solution)/shard_map/ppermute | solution.py:48
  93.9 29.7 %collective-permute-start.2 = (bf16[64,768]{1,0:T(8,128)(2,1)}, bf16[64,768]{1,0:T(8,128)(2,1)S(1)}, u32[]{:S(2)}, u32[]{:S(2)}) collective-permute-start(bf16[64,768]{1,0:T(8,128)(2,1)} %bitcast.201), channel_id=1, source_target_pairs={{0,12},{4,8},{8,4},{12,0},{16,28},{20,24},{24,20},{28,16},{1,13},{... | collective-permute-start | bytes 294920 | tf_op jit(solution)/shard_map/ppermute | solution.py:48
  106.3 25.1 %collective-permute-start.29 = (bf16[4,128,2048]{2,1,0:T(8,128)(2,1)}, bf16[4,128,2048]{2,1,0:T(8,128)(2,1)}, u32[]{:S(2)}, u32[]{:S(2)}) collective-permute-start(bf16[4,128,2048]{2,1,0:T(8,128)(2,1)} %pad_maximum_fusion.1), channel_id=1, source_target_pairs={{0,4},{4,0},{8,12},{12,8},{16,20},{20,16},{24,28},{28,24},{1,5},{5... | collective-permute-start | bytes 6291464 | tf_op jit(solution)/shard_map/ppermute | solution.py:48
  119.4 21.0 %collective-permute-start.16 = (bf16[4,128,2048]{2,1,0:T(8,128)(2,1)S(1)}, bf16[4,128,2048]{2,1,0:T(8,128)(2,1)S(1)}, u32[]{:S(2)}, u32[]{:S(2)}) collective-permute-start(bf16[4,128,2048]{2,1,0:T(8,128)(2,1)S(1)} %pad_maximum_fusion), channel_id=1, source_target_pairs={{0,4},{4,0},{8,12},{12,8},{16,20},{20,16},{24,28},{28,24},{1,5},{5... | collective-permute-start | bytes 6291464 | tf_op jit(solution)/shard_map/ppermute | solution.py:48
  147.4 20.2 %collective-permute-start.20 = (bf16[8,32,768]{2,1,0:T(8,128)(2,1)S(1)}, bf16[8,32,768]{2,1,0:T(8,128)(2,1)S(1)}, u32[]{:S(2)}, u32[]{:S(2)}) collective-permute-start(bf16[8,32,768]{2,1,0:T(8,128)(2,1)S(1)} %get-tuple-element.43), channel_id=1, source_target_pairs={{3,2},{7,6},{11,10},{15,14},{19,18},{23,22},{27,26},{31,30}} | collective-permute-start | bytes 1179656 | tf_op jit(solution)/shard_map/ppermute | solution.py:480
  180.3 18.8 %collective-permute-start.19 = (bf16[8,32,768]{2,1,0:T(8,128)(2,1)S(1)}, bf16[8,32,768]{2,1,0:T(8,128)(2,1)S(1)}, u32[]{:S(2)}, u32[]{:S(2)}) collective-permute-start(bf16[8,32,768]{2,1,0:T(8,128)(2,1)S(1)} %get-tuple-element.40), channel_id=1, source_target_pairs={{0,1},{1,2},{2,3},{4,5},{5,6},{6,7},{8,9},{9,10},{10,11},{12,13},{... | collective-permute-start | bytes 1179656 | tf_op jit(solution)/shard_map/ppermute | solution.py:480
  186.4 18.4 %collective-permute-start.22 = (bf16[8,32,768]{2,1,0:T(8,128)(2,1)S(1)}, bf16[8,32,768]{2,1,0:T(8,128)(2,1)S(1)}, u32[]{:S(2)}, u32[]{:S(2)}) collective-permute-start(bf16[8,32,768]{2,1,0:T(8,128)(2,1)S(1)} %fusion.42), channel_id=1, source_target_pairs={{1,0},{2,1},{3,2},{5,4},{6,5},{7,6},{9,8},{10,9},{11,10},{13,12},{... | collective-permute-start | bytes 1179656 | tf_op jit(solution)/shard_map/ppermute | solution.py:480
  214.8 32.9 %collective-permute-start.37 = (bf16[2,264,768]{2,1,0:T(8,128)(2,1)S(1)}, bf16[2,264,768]{2,1,0:T(8,128)(2,1)S(1)}, u32[]{:S(2)}, u32[]{:S(2)}) collective-permute-start(bf16[2,264,768]{2,1,0:T(8,128)(2,1)S(1)} %pad_maximum_fusion.8), channel_id=1, source_target_pairs={{0,16},{4,12},{8,24},{12,4},{16,0},{20,28},{24,8},{28,20},{1,17},{... | collective-permute-start | bytes 2433032 | tf_op jit(solution)/shard_map/ppermute | solution.py:48
  215.9 28.4 %collective-permute-start.54 = (bf16[264,768]{1,0:T(8,128)(2,1)S(1)}, bf16[264,768]{1,0:T(8,128)(2,1)S(1)}, u32[]{:S(2)}, u32[]{:S(2)}) collective-permute-start(bf16[264,768]{1,0:T(8,128)(2,1)S(1)} %convolution_convert_fusion.1), channel_id=1, source_target_pairs={{0,2},{1,3},{2,0},{3,1},{4,6},{5,7},{6,4},{7,5},{8,10},{9,11},{10,... | collective-permute-start | bytes 1216520 | tf_op jit(solution)/shard_map/ppermute | solution.py:517
  218.0 28.2 %collective-permute-start.64 = (bf16[1,264,768]{2,1,0:T(8,128)(2,1)S(1)}, bf16[1,264,768]{2,1,0:T(8,128)(2,1)S(1)}, u32[]{:S(2)}, u32[]{:S(2)}) collective-permute-start(bf16[1,264,768]{2,1,0:T(8,128)(2,1)S(1)} %bitcast.220), channel_id=1, source_target_pairs={{0,8},{4,20},{8,0},{12,28},{16,24},{20,4},{24,16},{28,12},{1,9},{5... | collective-permute-start | bytes 1216520 | tf_op jit(solution)/shard_map/ppermute | solution.py:48
  219.7 29.5 %collective-permute-start.45 = (bf16[264,768]{1,0:T(8,128)(2,1)S(1)}, bf16[264,768]{1,0:T(8,128)(2,1)S(1)}, u32[]{:S(2)}, u32[]{:S(2)}) collective-permute-start(bf16[264,768]{1,0:T(8,128)(2,1)S(1)} %convolution_convert_fusion.2), channel_id=1, source_target_pairs={{0,1},{1,2},{2,3},{3,0},{4,5},{5,6},{6,7},{7,4},{8,9},{9,10},{10,1... | collective-permute-start | bytes 1216520 | tf_op jit(solution)/shard_map/ppermute | solution.py:517
  247.2 25.9 %collective-permute-start.65 = (bf16[2,264,768]{2,1,0:T(8,128)(2,1)}, bf16[2,264,768]{2,1,0:T(8,128)(2,1)}, u32[]{:S(2)}, u32[]{:S(2)}) collective-permute-start(bf16[2,264,768]{2,1,0:T(8,128)(2,1)} %pad_maximum_fusion.11), channel_id=1, source_target_pairs={{0,16},{4,12},{8,24},{12,4},{16,0},{20,28},{24,8},{28,20},{1,17},{... | collective-permute-start | bytes 2433032 | tf_op jit(solution)/shard_map/ppermute | solution.py:48
  249.2 53.7 %collective-permute-start.38 = (bf16[4,264,768]{2,1,0:T(8,128)(2,1)}, bf16[4,264,768]{2,1,0:T(8,128)(2,1)}, u32[]{:S(2)}, u32[]{:S(2)}) collective-permute-start(bf16[4,264,768]{2,1,0:T(8,128)(2,1)} %pad_maximum_fusion.2), channel_id=1, source_target_pairs={{0,4},{4,0},{8,12},{12,8},{16,20},{20,16},{24,28},{28,24},{1,5},{5... | collective-permute-start | bytes 4866056 | tf_op jit(solution)/shard_map/ppermute | solution.py:48
  257.4 41.0 %collective-permute-start.56 = (bf16[2,264,768]{2,1,0:T(8,128)(2,1)}, bf16[2,264,768]{2,1,0:T(8,128)(2,1)}, u32[]{:S(2)}, u32[]{:S(2)}) collective-permute-start(bf16[2,264,768]{2,1,0:T(8,128)(2,1)} %pad_maximum_fusion.10), channel_id=1, source_target_pairs={{0,16},{4,12},{8,24},{12,4},{16,0},{20,28},{24,8},{28,20},{1,17},{... | collective-permute-start | bytes 2433032 | tf_op jit(solution)/shard_map/ppermute | solution.py:48
  266.2 34.8 %collective-permute-start.47 = (bf16[2,264,768]{2,1,0:T(8,128)(2,1)}, bf16[2,264,768]{2,1,0:T(8,128)(2,1)}, u32[]{:S(2)}, u32[]{:S(2)}) collective-permute-start(bf16[2,264,768]{2,1,0:T(8,128)(2,1)} %pad_maximum_fusion.9), channel_id=1, source_target_pairs={{0,16},{4,12},{8,24},{12,4},{16,0},{20,28},{24,8},{28,20},{1,17},{... | collective-permute-start | bytes 2433032 | tf_op jit(solution)/shard_map/ppermute | solution.py:48
  274.5 59.1 %collective-permute-start.66 = (bf16[4,264,768]{2,1,0:T(8,128)(2,1)S(1)}, bf16[4,264,768]{2,1,0:T(8,128)(2,1)S(1)}, u32[]{:S(2)}, u32[]{:S(2)}) collective-permute-start(bf16[4,264,768]{2,1,0:T(8,128)(2,1)S(1)} %pad_maximum_fusion.5), channel_id=1, source_target_pairs={{0,4},{4,0},{8,12},{12,8},{16,20},{20,16},{24,28},{28,24},{1,5},{5... | collective-permute-start | bytes 4866056 | tf_op jit(solution)/shard_map/ppermute | solution.py:48
  300.9 63.6 %collective-permute-start.57 = (bf16[4,264,768]{2,1,0:T(8,128)(2,1)}, bf16[4,264,768]{2,1,0:T(8,128)(2,1)S(1)}, u32[]{:S(2)}, u32[]{:S(2)}) collective-permute-start(bf16[4,264,768]{2,1,0:T(8,128)(2,1)} %pad_maximum_fusion.4), channel_id=1, source_target_pairs={{0,4},{4,0},{8,12},{12,8},{16,20},{20,16},{24,28},{28,24},{1,5},{5... | collective-permute-start | bytes 4866056 | tf_op jit(solution)/shard_map/ppermute | solution.py:48
  302.3 93.1 %collective-permute-start.48 = (bf16[4,264,768]{2,1,0:T(8,128)(2,1)S(1)}, bf16[4,264,768]{2,1,0:T(8,128)(2,1)S(1)}, u32[]{:S(2)}, u32[]{:S(2)}) collective-permute-start(bf16[4,264,768]{2,1,0:T(8,128)(2,1)S(1)} %pad_maximum_fusion.3), channel_id=1, source_target_pairs={{0,4},{4,0},{8,12},{12,8},{16,20},{20,16},{24,28},{28,24},{1,5},{5... | collective-permute-start | bytes 4866056 | tf_op jit(solution)/shard_map/ppermute | solution.py:48
  333.5 88.8 %collective-permute-start.42 = (bf16[4,264,768]{2,1,0:T(8,128)(2,1)}, bf16[4,264,768]{2,1,0:T(8,128)(2,1)}, u32[]{:S(2)}, u32[]{:S(2)}) collective-permute-start(bf16[4,264,768]{2,1,0:T(8,128)(2,1)} %get-tuple-element.18), channel_id=1, source_target_pairs={{0,4},{4,0},{8,12},{12,8},{16,20},{20,16},{24,28},{28,24},{1,5},{5... | collective-permute-start | bytes 4866056 | tf_op jit(solution)/shard_map/ppermute | solution.py:48
  364.1 61.0 %collective-permute-start.68 = (bf16[4,264,768]{2,1,0:T(8,128)(2,1)}, bf16[4,264,768]{2,1,0:T(8,128)(2,1)}, u32[]{:S(2)}, u32[]{:S(2)}) collective-permute-start(bf16[4,264,768]{2,1,0:T(8,128)(2,1)} %get-tuple-element.24), channel_id=1, source_target_pairs={{0,4},{4,0},{8,12},{12,8},{16,20},{20,16},{24,28},{28,24},{1,5},{5... | collective-permute-start | bytes 4866056 | tf_op jit(solution)/shard_map/ppermute | solution.py:48
  395.4 32.9 %collective-permute-start.59 = (bf16[4,264,768]{2,1,0:T(8,128)(2,1)}, bf16[4,264,768]{2,1,0:T(8,128)(2,1)}, u32[]{:S(2)}, u32[]{:S(2)}) collective-permute-start(bf16[4,264,768]{2,1,0:T(8,128)(2,1)} %get-tuple-element.22), channel_id=1, source_target_pairs={{0,4},{4,0},{8,12},{12,8},{16,20},{20,16},{24,28},{28,24},{1,5},{5... | collective-permute-start | bytes 4866056 | tf_op jit(solution)/shard_map/ppermute | solution.py:48
  427.3 22.2 %collective-permute-start.69 = (bf16[2,264,768]{2,1,0:T(8,128)(2,1)S(1)}, bf16[2,264,768]{2,1,0:T(8,128)(2,1)S(1)}, u32[]{:S(2)}, u32[]{:S(2)}) collective-permute-start(bf16[2,264,768]{2,1,0:T(8,128)(2,1)S(1)} %slice.193), channel_id=1, source_target_pairs={{0,16},{4,12},{8,24},{12,4},{16,0},{20,28},{24,8},{28,20},{1,17},{... | collective-permute-start | bytes 2433032 | tf_op jit(solution)/shard_map/ppermute | solution.py:48
  430.5 32.0 %collective-permute-start.60 = (bf16[2,264,768]{2,1,0:T(8,128)(2,1)S(1)}, bf16[2,264,768]{2,1,0:T(8,128)(2,1)S(1)}, u32[]{:S(2)}, u32[]{:S(2)}) collective-permute-start(bf16[2,264,768]{2,1,0:T(8,128)(2,1)S(1)} %slice.194), channel_id=1, source_target_pairs={{0,16},{4,12},{8,24},{12,4},{16,0},{20,28},{24,8},{28,20},{1,17},{... | collective-permute-start | bytes 2433032 | tf_op jit(solution)/shard_map/ppermute | solution.py:48
  432.3 43.2 %collective-permute-start.51 = (bf16[2,264,768]{2,1,0:T(8,128)(2,1)S(1)}, bf16[2,264,768]{2,1,0:T(8,128)(2,1)S(1)}, u32[]{:S(2)}, u32[]{:S(2)}) collective-permute-start(bf16[2,264,768]{2,1,0:T(8,128)(2,1)S(1)} %slice.195), channel_id=1, source_target_pairs={{0,16},{4,12},{8,24},{12,4},{16,0},{20,28},{24,8},{28,20},{1,17},{... | collective-permute-start | bytes 2433032 | tf_op jit(solution)/shard_map/ppermute | solution.py:48
  436.7 40.8 %collective-permute-start.44 = (bf16[1,264,768]{2,1,0:T(8,128)(2,1)S(1)}, bf16[1,264,768]{2,1,0:T(8,128)(2,1)S(1)}, u32[]{:S(2)}, u32[]{:S(2)}) collective-permute-start(bf16[1,264,768]{2,1,0:T(8,128)(2,1)S(1)} %slice.200), channel_id=1, source_target_pairs={{0,8},{4,20},{8,0},{12,28},{16,24},{20,4},{24,16},{28,12},{1,9},{5... | collective-permute-start | bytes 1216520 | tf_op jit(solution)/shard_map/ppermute | solution.py:48
  449.7 29.6 %collective-permute-start.70 = (bf16[1,264,768]{2,1,0:T(8,128)(2,1)S(1)}, bf16[1,264,768]{2,1,0:T(8,128)(2,1)S(1)}, u32[]{:S(2)}, u32[]{:S(2)}) collective-permute-start(bf16[1,264,768]{2,1,0:T(8,128)(2,1)S(1)} %slice.197), channel_id=1, source_target_pairs={{0,8},{4,20},{8,0},{12,28},{16,24},{20,4},{24,16},{28,12},{1,9},{5... | collective-permute-start | bytes 1216520 | tf_op jit(solution)/shard_map/ppermute | solution.py:48
  479.2 26.4 %collective-permute-start.62 = (bf16[264,768]{1,0:T(8,128)(2,1)S(1)}, bf16[264,768]{1,0:T(8,128)(2,1)S(1)}, u32[]{:S(2)}, u32[]{:S(2)}) collective-permute-start(bf16[264,768]{1,0:T(8,128)(2,1)S(1)} %fusion.54), channel_id=1, source_target_pairs={{2,0},{3,1},{0,2},{1,3},{6,4},{7,5},{4,6},{5,7},{10,8},{11,9},{8,1... | collective-permute-start | bytes 1216520 | tf_op jit(solution)/shard_map/ppermute | solution.py:525
  479.4 32.4 %collective-permute-start.71 = (bf16[264,768]{1,0:T(8,128)(2,1)S(1)}, bf16[264,768]{1,0:T(8,128)(2,1)S(1)}, u32[]{:S(2)}, u32[]{:S(2)}) collective-permute-start(bf16[264,768]{1,0:T(8,128)(2,1)S(1)} %fusion.55), channel_id=1, source_target_pairs={{3,0},{0,1},{1,2},{2,3},{7,4},{4,5},{5,6},{6,7},{11,8},{8,9},{9,10... | collective-permute-start | bytes 1216520 | tf_op jit(solution)/shard_map/ppermute | solution.py:525
  483.8 26.5 %collective-permute-start.53 = (bf16[264,768]{1,0:T(8,128)(2,1)S(1)}, bf16[264,768]{1,0:T(8,128)(2,1)S(1)}, u32[]{:S(2)}, u32[]{:S(2)}) collective-permute-start(bf16[264,768]{1,0:T(8,128)(2,1)S(1)} %fusion.53), channel_id=1, source_target_pairs={{1,0},{2,1},{3,2},{0,3},{5,4},{6,5},{7,6},{4,7},{9,8},{10,9},{11,1... | collective-permute-start | bytes 1216520 | tf_op jit(solution)/shard_map/ppermute | solution.py:525
  (83 other events, 707.0 us)

commit v2 on v1

v2 whole, which is shorter than its diff:
```python
import functools

import jax
import jax.numpy as jnp
from jax import lax
from jax.experimental import pallas as pl
from jax.experimental.pallas import tpu as pltpu
from jax.sharding import PartitionSpec as P

MIB = 1 << 20
BF = jnp.bfloat16
F32 = jnp.float32


def routes(count):
    bits = [1 << b for b in range(1, count.bit_length() - 1)]
    turn = len(bits) // 2
    return bits, bits[turn:] + bits[:turn]


def hop(count, step):
    both = routes(count)
    return [(i, i ^ both[i & 1][step]) for i in range(count)]


def hop_mask(count, step, side):
    both = routes(count)
    return jnp.where(side == 0, both[0][step], both[1][step])


def pair(count):
    return [(i, i ^ 1) for i in range(count)]


def held_by(count, who):
    held = [who]
    for step in range(len(routes(count)[0])):
        mask = hop_mask(count, step, who & 1)
        held = held + [h ^ mask for h in held]
    return held


def block_order(count, me):
    return held_by(count, me) + held_by(count, me ^ 1)


def send(x, perm):
    return lax.ppermute(x, "ctx", perm)


def after(x, *others):
    return lax.optimization_barrier((x, *others))[0]


def joined(parts):
    return parts[0] if len(parts) == 1 else jnp.concatenate(parts, axis=0)


def spread(x, count, gates=()):
    pieces = [x[None]]
    for step in range(len(routes(count)[0])):
        block = joined(pieces)
        if step < len(gates):
            block = after(block, *gates[step])
        pieces.append(send(block, hop(count, step)))
    block = tuple(pieces)
    if len(gates) > len(routes(count)[0]):
        block = after(block, *gates[-1])
    return pieces + [send(x, pair(count)) for x in block]


def pair_sum(near, far, count):
    return (near.astype(F32) + send(far, pair(count)).astype(F32)).astype(BF)


def gathered_sum(total, count, gates=()):
    got = []
    for at, step in enumerate(reversed(range(len(routes(count)[0])))):
        half = total.shape[0] // 2
        leaving = total[half:]
        if at < len(gates):
            leaving = after(leaving, *gates[at])
        other = send(leaving, hop(count, step))
        got.append(other)
        total = (total[:half].astype(F32) + other.astype(F32)).astype(BF)
    return total[0], got


def sum_over(x, count):
    for bit in range(count.bit_length() - 1):
        x = x + send(x, [(i, i ^ (1 << bit)) for i in range(count)])
    return x


def swap_blocks(blocks, count):
    got = [blocks[0]]
    for j in range(1, count):
        got.append(send(blocks[j], [(i, i ^ j) for i in range(count)]))
    return got


def cut_kernel(mates_ref, x_ref, *outs):
    cols = outs[0].shape[1]
    for j, out in enumerate(outs):
        out[...] = x_ref[:, pl.ds(pl.multiple_of(mates_ref[j] * cols, cols), cols)]


def cut_columns(x, mates):
    rows, width = x.shape
    count = mates.shape[0]
    whole = pl.BlockSpec(memory_space=pltpu.VMEM)
    shape = jax.ShapeDtypeStruct((rows, width // count), x.dtype)
    return pl.pallas_call(
        cut_kernel,
        in_specs=[pl.BlockSpec(memory_space=pltpu.SMEM), whole],
        out_specs=[whole] * count,
        out_shape=[shape] * count,
    )(mates, x)


def lay_kernel(mates_ref, *refs):
    *blocks, out_ref = refs
    cols = blocks[0].shape[1]
    for j, ref in enumerate(blocks):
        out_ref[:, pl.ds(pl.multiple_of(mates_ref[j] * cols, cols), cols)] = ref[...]


def lay_columns(blocks, mates):
    rows, cols = blocks[0].shape
    whole = pl.BlockSpec(memory_space=pltpu.VMEM)
    return pl.pallas_call(
        lay_kernel,
        in_specs=[pl.BlockSpec(memory_space=pltpu.SMEM)] + [whole] * len(blocks),
        out_specs=whole,
        out_shape=jax.ShapeDtypeStruct((rows, cols * len(blocks)), blocks[0].dtype),
    )(mates, *blocks)


def state_kernel(dim, place_ref, k_ref, v_ref, cum_ref, out_ref):
    cum = cum_ref[...]
    fade = jnp.exp(cum[-1:, :] - cum)
    for h in range(cum.shape[1]):
        lanes = slice(h * dim, (h + 1) * dim)
        faded = (k_ref[0, :, lanes].astype(F32) * fade[:, h : h + 1]).astype(BF)
        out_ref[0, h] = lax.dot_general(
            faded, v_ref[0, :, lanes], (((0,), (0,)), ((), ())), preferred_element_type=F32
        ).astype(BF)


def local_states(keys, values, cum, place):
    seqs, block, width = keys.shape
    heads = cum.shape[1]
    dim = width // 2 // heads
    rows = pl.BlockSpec((1, block, width // 2), lambda s, place: (s, 0, place[0]))
    return pl.pallas_call(
        functools.partial(state_kernel, dim),
        grid_spec=pltpu.PrefetchScalarGridSpec(
            num_scalar_prefetch=1,
            grid=(seqs,),
            in_specs=[rows, rows, pl.BlockSpec((block, heads), lambda s, place: (0, 0))],
            out_specs=pl.BlockSpec((1, heads, dim, dim), lambda s, place: (s, 0, 0, 0)),
        ),
        out_shape=jax.ShapeDtypeStruct((seqs, heads, dim, dim), BF),
        compiler_params=pltpu.CompilerParams(vmem_limit_bytes=60 * MIB),
        cost_estimate=pl.CostEstimate(
            flops=2000000000, bytes_accessed=2 * seqs * width * (block + dim), transcendentals=0
        ),
    )(place.reshape(1).astype(jnp.int32), keys, values, cum)


def within_kernel(dim, q_ref, k_ref, v_ref, g_ref, cum_ref, cumt_ref, gain_ref, out_ref, act_ref):
    cum = cum_ref[...]
    block = cum.shape[0]
    causal = lax.broadcasted_iota(jnp.int32, (block, block), 0) >= lax.broadcasted_iota(
        jnp.int32, (block, block), 1
    )
    for h in range(cum.shape[1]):
        lanes = slice(h * dim, (h + 1) * dim)
        scores = lax.dot_general(
            q_ref[0, :, lanes],
            k_ref[0, :, lanes],
            (((1,), (1,)), ((), ())),
            preferred_element_type=F32,
        )
        gap = jnp.where(causal, cum[:, h : h + 1] - cumt_ref[h : h + 1, :], -1e30)
        weights = (scores * jnp.exp(gap)).astype(BF)
        out_ref[0, :, lanes] = jnp.dot(weights, v_ref[0, :, lanes], preferred_element_type=F32)
    act_ref[0] = gain_ref[...] * jax.nn.sigmoid(g_ref[0].astype(F32))


def within_block(queries, keys, values, gate, cum, head_gain):
    seqs, block, width = keys.shape
    heads = cum.shape[1]
    dim = width // heads
    rows = pl.BlockSpec((1, block, width), lambda s: (s, 0, 0))
    shape = jax.ShapeDtypeStruct((seqs, block, width), F32)
    return pl.pallas_call(
        functools.partial(within_kernel, dim),
        grid=(seqs,),
        in_specs=[
            rows,
            rows,
            rows,
            rows,
            pl.BlockSpec((block, heads), lambda s: (0, 0)),
            pl.BlockSpec((heads, block), lambda s: (0, 0)),
            pl.BlockSpec((1, width), lambda s: (0, 0)),
        ],
        out_specs=[rows, rows],
        out_shape=[shape, shape],
        compiler_params=pltpu.CompilerParams(vmem_limit_bytes=60 * MIB),
        cost_estimate=pl.CostEstimate(
            flops=60 * seqs * block * block * width,
            bytes_accessed=16 * seqs * block * width,
            transcendentals=seqs * block * width,
        ),
    )(queries, keys, values, gate, cum, cum.T, head_gain[None])


def combine_kernel(weight_ref, *refs):
    *states, out_ref = refs
    for h in range(out_ref.shape[1]):
        out_ref[0, h] = sum(
            weight_ref[i, h] * ref[0, h].astype(F32) for i, ref in enumerate(states)
        ).astype(BF)


def combine(states, weights):
    seqs, heads, dim, _ = states[0].shape
    block = pl.BlockSpec((1, heads, dim, dim), lambda s: (s, 0, 0, 0))
    return pl.pallas_call(
        combine_kernel,
        grid=(seqs,),
        in_specs=[pl.BlockSpec(memory_space=pltpu.SMEM)] + [block] * len(states),
        out_specs=block,
        out_shape=jax.ShapeDtypeStruct(states[0].shape, BF),
        compiler_params=pltpu.CompilerParams(vmem_limit_bytes=16 * MIB),
    )(weights, *states)


def mixed_kernel(
    dim, sub, side_ref, weight_ref, q_ref, own_ref, got_ref, pair_own_ref, pair_got_ref,
    within_ref, act_ref, cum_ref, out_ref,
):
    scale = jnp.exp(cum_ref[...])
    heads = scale.shape[1]
    half = heads // 2
    for h in range(heads):
        lanes = slice(h * dim, (h + 1) * dim)
        here = side_ref[0] == h // half
        entering = jnp.where(here, own_ref[0, h % half], got_ref[0, h % half]).astype(F32)
        paired = jnp.where(here, pair_own_ref[0, h % half], pair_got_ref[0, h % half]).astype(F32)
        state = (weight_ref[0, h] * entering + weight_ref[1, h] * paired).astype(BF)
        carried = jnp.dot(q_ref[0, :, lanes], state, preferred_element_type=F32)
        attended = within_ref[0, :, lanes] + carried * scale[:, h : h + 1]
        square = jnp.mean(attended * attended, axis=1, keepdims=True)
        mixed = (attended * lax.rsqrt(square + 1e-06) * act_ref[0, :, lanes]).astype(BF)
        for d in range(out_ref.shape[0]):
            out_ref[d, 0, :, lanes] = mixed[d * sub : (d + 1) * sub]


def mixed_rows(queries, states, weights, side, within, act, cum, sub, first, seqs):
    _, block, width = queries.shape
    heads = cum.shape[1]
    dim = width // heads
    parts = block // sub
    rows = pl.BlockSpec((1, block, width), lambda s, side: (s + first, 0, 0))
    halved = pl.BlockSpec((1, heads // 2, dim, dim), lambda s, side: (s + first, 0, 0, 0))
    return pl.pallas_call(
        functools.partial(mixed_kernel, dim, sub),
        grid_spec=pltpu.PrefetchScalarGridSpec(
            num_scalar_prefetch=1,
            grid=(seqs,),
            in_specs=[pl.BlockSpec(memory_space=pltpu.SMEM), rows]
            + [halved] * 4
            + [rows, rows, pl.BlockSpec((block, heads), lambda s, side: (0, 0))],
            out_specs=pl.BlockSpec((parts, 1, sub, width), lambda s, side: (0, s, 0, 0)),
        ),
        out_shape=jax.ShapeDtypeStruct((parts, seqs, sub, width), BF),
        compiler_params=pltpu.CompilerParams(vmem_limit_bytes=60 * MIB),
        cost_estimate=pl.CostEstimate(
            flops=6000000000, bytes_accessed=14 * seqs * block * width, transcendentals=0
        ),
    )(side.reshape(1).astype(jnp.int32), weights, queries, *states, within, act, cum)


def project_kernel(sizes, order_ref, *refs):
    *pieces, w_ref, out_ref = refs
    parts, _, rows, _ = out_ref.shape
    at = 0
    for ref, size in zip(pieces, sizes):
        for i in range(size):
            product = jnp.dot(ref[i], w_ref[...], preferred_element_type=F32).astype(BF)
            for d in range(parts):
                out_ref[d, order_ref[at]] = product[d * rows : (d + 1) * rows]
            at += 1


def project(pieces, weight, order, parts):
    count = sum(p.shape[0] for p in pieces)
    rows, depth = pieces[0].shape[1:]
    cols = weight.shape[1]
    whole = pl.BlockSpec(memory_space=pltpu.VMEM)
    return pl.pallas_call(
        functools.partial(project_kernel, [p.shape[0] for p in pieces]),
        in_specs=[pl.BlockSpec(memory_space=pltpu.SMEM)] + [whole] * (len(pieces) + 1),
        out_specs=whole,
        out_shape=jax.ShapeDtypeStruct((parts, count, rows // parts, cols), BF),
        compiler_params=pltpu.CompilerParams(vmem_limit_bytes=20 * MIB),
        cost_estimate=pl.CostEstimate(
            flops=4 * count * rows * depth * cols,
            bytes_accessed=2 * (count * rows * (depth + cols) + depth * cols),
            transcendentals=0,
        ),
    )(order, *pieces, weight)


def residual_kernel(count, mates_ref, *refs):
    stream, sums = refs[:count], refs[count:-2]
    out_ref, square_ref = refs[-2:]
    rows = out_ref.shape[1] // len(sums)
    for j in range(count):
        out_ref[mates_ref[j]] = stream[j][...].astype(F32)
    for b in range(count):
        for h, ref in enumerate(sums):
            at = slice(h * rows, (h + 1) * rows)
            total = out_ref[b, at] + ref[b].astype(F32)
            out_ref[b, at] = total
            square_ref[b, at] = jnp.sum(total * total, axis=1, keepdims=True)


def residual_sums(mates, stream, sums):
    count = len(stream)
    rows, cols = stream[0].shape
    whole = pl.BlockSpec(memory_space=pltpu.VMEM)
    return pl.pallas_call(
        functools.partial(residual_kernel, count),
        in_specs=[pl.BlockSpec(memory_space=pltpu.SMEM)] + [whole] * (count + len(sums)),
        out_specs=[whole] * 2,
        out_shape=[
            jax.ShapeDtypeStruct((count, rows, cols), F32),
            jax.ShapeDtypeStruct((count, rows, 1), F32),
        ],
        compiler_params=pltpu.CompilerParams(vmem_limit_bytes=32 * MIB),
    )(mates, *stream, *sums)


def hidden_kernel(sizes, groups, order_ref, *refs):
    steps = sum(sizes)
    each = len(sizes)
    pieces = [refs[g * each : (g + 1) * each] for g in range(groups)]
    refs = refs[groups * each :]
    (gate_ref, up_ref), outs = refs[:2], refs[2:]
    outs, g_acc, u_acc = outs[:groups], outs[-2], outs[-1]
    i = pl.program_id(0)

    start = 0
    for p, size in enumerate(sizes):

        @pl.when((i >= start) & (i < start + size))
        def _(p=p, start=start):
            for g in range(groups):
                rows = pieces[g][p][0]
                gate = jnp.dot(rows, gate_ref[...], preferred_element_type=F32)
                up = jnp.dot(rows, up_ref[...], preferred_element_type=F32)
                if start == 0:
                    g_acc[g] = gate
                    u_acc[g] = up
                else:
                    g_acc[g] += gate
                    u_acc[g] += up

        start += size

    @pl.when(i == steps - 1)
    def _():
        for g in range(groups):
            v = g_acc[g]
            outs[g][...] = (v / (1.0 + jnp.exp(-v)) * u_acc[g]).astype(BF)


def hidden_units(groups, w_gate, w_up, order):
    sizes = [p.shape[0] for p in groups[0]]
    rows, cols = groups[0][0].shape[1:]
    depth, hid = w_gate.shape
    many = len(groups)
    specs = []
    start = 0
    for size in sizes:
        specs.append(
            pl.BlockSpec(
                (1, rows, cols),
                lambda i, order, start=start, size=size: (jnp.clip(i - start, 0, size - 1), 0, 0),
            )
        )
        start += size
    up_spec = pl.BlockSpec((cols, hid), lambda i, order: (order[i], 0))
    return pl.pallas_call(
        functools.partial(hidden_kernel, sizes, many),
        grid_spec=pltpu.PrefetchScalarGridSpec(
            num_scalar_prefetch=1,
            grid=(sum(sizes),),
            in_specs=specs * many
            + [up_spec, up_spec],
            out_specs=[pl.BlockSpec((rows, hid), lambda i, order: (0, 0))] * many,
            scratch_shapes=[pltpu.VMEM((many, rows, hid), F32)] * 2,
        ),
        out_shape=[jax.ShapeDtypeStruct((rows, hid), BF)] * many,
        compiler_params=pltpu.CompilerParams(vmem_limit_bytes=60 * MIB),
        cost_estimate=pl.CostEstimate(
            flops=8 * many * rows * depth * hid,
            bytes_accessed=4 * depth * hid + 2 * many * rows * depth,
            transcendentals=many * rows * hid,
        ),
    )(order, *[p for pieces in groups for p in pieces], w_gate, w_up)


def down_kernel(groups, order_ref, *refs):
    hidden, weight, outs = refs[:groups], refs[groups], refs[groups + 1 :]
    for g in range(groups):
        outs[g][0] = jnp.dot(hidden[g][...], weight[...], preferred_element_type=F32).astype(BF)


def down_blocks(hidden, w_down, order):
    many = len(hidden)
    rows, hid = hidden[0].shape
    blocks, model = order.shape[0], w_down.shape[1]
    cols = model // lax.axis_size("ctx")

    return pl.pallas_call(
        functools.partial(down_kernel, many),
        grid_spec=pltpu.PrefetchScalarGridSpec(
            num_scalar_prefetch=1,
            grid=(blocks,),
            in_specs=[pl.BlockSpec((rows, hid), lambda i, order: (0, 0))] * many
            + [pl.BlockSpec((hid, cols), lambda i, order: (0, order[i]))],
            out_specs=[pl.BlockSpec((1, rows, cols), lambda i, order: (i, 0, 0))] * many,
        ),
        out_shape=[jax.ShapeDtypeStruct((blocks, rows, cols), BF)] * many,
        compiler_params=pltpu.CompilerParams(vmem_limit_bytes=60 * MIB),
        cost_estimate=pl.CostEstimate(
            flops=4 * many * rows * cols * blocks * hid,
            bytes_accessed=2 * cols * blocks * hid + 2 * many * rows * cols * blocks,
            transcendentals=0,
        ),
    )(order, *hidden, w_down)


def body(
    queries,
    keys,
    values,
    decay_log,
    out_gate,
    head_gain,
    out_weight,
    stream,
    norm_gain,
    expert_ids,
    expert_share,
    w_gate,
    w_up,
    w_down,
):
    count = lax.axis_size("ctx")
    parts = lax.axis_size("exp")
    me = lax.axis_index("ctx")
    mine = lax.axis_index("exp")
    side = me & 1
    seqs, block, width = queries.shape
    heads = decay_log.shape[1]
    sub, model = stream.shape[1:]
    tokens = seqs * sub
    cols = model // count
    order = block_order(count, me)
    order_array = jnp.stack(order).astype(jnp.int32)

    cum = jnp.cumsum(decay_log, axis=0)
    small = jnp.concatenate(
        [
            expert_ids.reshape(2 * tokens).astype(F32),
            expert_share.reshape(2 * tokens),
            cum[-1],
        ]
    )
    width_small = small.shape[0]
    small = jnp.pad(small, (0, -width_small % 128)).reshape(-1, 128)
    facts = joined(spread(small, count)).reshape(count, -1)
    steps = len(routes(count)[0])
    place = order_array[None, :] == jnp.arange(count, dtype=jnp.int32)[:, None]
    facts = jnp.sum(jnp.where(place[:, :, None], facts[None], 0.0), axis=1)
    ids = facts[:, : 2 * tokens].astype(jnp.int32)
    shares = facts[:, 2 * tokens : 4 * tokens]
    ends = facts[:, 4 * tokens : 4 * tokens + heads]

    mates = (me ^ jnp.arange(count, dtype=jnp.int32)).astype(jnp.int32)

    block_no = jnp.arange(count)

    def faded(source, target):
        between = (block_no >= 2 * (source // 2 + 1)) & (block_no < 2 * (target // 2))
        power = jnp.sum(jnp.where(between[:, None], ends, 0.0), axis=0)
        return jnp.where(source // 2 < target // 2, jnp.exp(power), 0.0)

    half_heads = heads // 2

    def side_half(row):
        return lax.dynamic_slice_in_dim(row, side * half_heads, half_heads, 0)

    fade_own = jnp.exp(cum[-1])
    lanes = jnp.pad(cum[-1:], ((0, 0), (0, -heads % 128)))
    fade_other = jnp.exp(send(lanes, pair(count))[0, :heads])
    ones = jnp.ones_like(fade_own)
    chip_weights = jnp.stack(
        [
            side_half(jnp.where(side == 0, fade_other, ones)),
            side_half(jnp.where(side == 0, ones, fade_own)),
        ]
    )
    enter_weights = jnp.stack(
        [jnp.where(side == 0, ones, fade_other), jnp.where(side == 0, 0.0, ones)]
    )

    cum_mine = lax.dynamic_slice_in_dim(cum, side * half_heads, half_heads, 1)
    cum_theirs = lax.dynamic_slice_in_dim(cum, (1 - side) * half_heads, half_heads, 1)
    state_theirs = local_states(keys, values, cum_theirs, 1 - side)
    state_mine = local_states(keys, values, cum_mine, side)
    other_mine = send(state_theirs, pair(count))
    other_theirs = send(state_mine, pair(count))
    chip = combine([state_mine, other_mine], chip_weights)
    within, act = within_block(queries, keys, values, out_gate, after(cum, chip), head_gain)
    held, names = [chip], [me]
    for step in range(steps - 1):
        got = send(jnp.stack(held) if step else held[0][None], hop(count, step))
        mask = hop_mask(count, step, side)
        held = held + [got[i] for i in range(len(held))]
        names = names + [name ^ mask for name in names]
    there = me ^ hop_mask(count, steps - 1, side)
    towards = [jnp.stack([side_half(faded(name, t)) for name in names]) for t in (there, me)]
    got = send(combine(held, after(towards[0], within)), hop(count, steps - 1))
    alone = jnp.concatenate([towards[1], jnp.ones((1, half_heads), F32)])
    entering = combine(held + [got], alone)
    states = [entering, send(entering, pair(count)), other_mine, other_theirs]
    halves = 2
    each = seqs // halves
    mixed = [
        mixed_rows(
            queries, states, enter_weights, side, within, act, cum, sub, h * each, each
        ).reshape(parts * each * sub, width)
        for h in range(halves)
    ]

    summed = []
    gates = [(), tuple(mixed[1:])]
    for h in range(halves):
        pieces = spread(mixed[h], count, gates)
        partial = project(pieces, out_weight, order_array, parts)
        gates = [(pieces[1],)] + [()] * (steps - 1) + [(partial,)]
        summed.append(lax.psum_scatter(partial, "exp", scatter_dimension=0))

    stream_rows = after(stream, partial).reshape(tokens, model)
    stream_got = swap_blocks(cut_columns(stream_rows, mates), count)
    residual, square = residual_sums(mates, stream_got, summed)
    residual = residual.reshape(count * tokens, cols)

    square = sum_over(square.reshape(count * tokens), count)
    scale = lax.rsqrt(square / model + 1e-06)
    gain = lax.dynamic_slice_in_dim(norm_gain, me * cols, cols, 0)
    rows_in = (residual * scale[:, None] * gain).astype(BF)

    expert_local = w_gate.shape[0]
    experts = expert_local * parts
    capacity = max(2, (2 * tokens + experts - 1) // experts + 1)
    one_hot = ids[:, :, None] == jnp.arange(experts, dtype=jnp.int32)
    earlier = jnp.arange(2 * tokens)[:, None] > jnp.arange(2 * tokens)[None, :]
    ahead = jnp.einsum(
        "tu,gue->gte", earlier.astype(BF), one_hot.astype(BF), preferred_element_type=F32
    )
    ranking = jnp.sum(jnp.where(one_hot, ahead, 0.0), axis=2).astype(jnp.int32)
    slots = capacity * count
    turned = (ids - mine + experts) % experts
    slot_of = (turned * count + jnp.arange(count, dtype=jnp.int32)[:, None]) * capacity + ranking
    slot_of = slot_of.reshape(count * tokens, 2)
    share_of = shares.reshape(count * tokens, 2)
    sent = []
    for turn in range(parts):
        numbers = turn * slots + jnp.arange(slots, dtype=jnp.int32)
        hit = [slot_of[:, k][None, :] == numbers[:, None] for k in range(2)]
        placing = hit[0] | hit[1]
        dispatch = jnp.dot(placing.astype(BF), rows_in, preferred_element_type=F32).astype(BF)
        if turn:
            dispatch = lax.ppermute(dispatch, "exp", [(i, (i + turn) % parts) for i in range(parts)])
        sent.append(dispatch)

    arrived = []
    for turn in range(parts):
        gates = [()] * steps
        if turn == 0:
            gates[-1] = (sent[1],)
        elif turn == 1:
            gates[-1] = (arrived[0][steps], sent[2 % parts])
            gates.append((sent[3 % parts],))
        else:
            gates[0] = (arrived[0 if turn < 4 else turn - 2][steps],)
        arrived.append(spread(sent[turn], count, gates))
    near_order, far_order = order_array[: count // 2], order_array[count // 2 :]
    returned = []
    waits, moved = [], [[]] * steps
    for first in range(0, parts, 2):
        turns = range(first, min(first + 2, parts))
        later = range(first + 2, min(first + 4, parts))
        ready = [arrived[t][1] for t in later]
        groups = [arrived[t] for t in turns]
        groups[0] = list(after(tuple(groups[0]), *waits, *ready))
        hidden = hidden_units(groups, w_gate[0], w_up[0], order_array)
        ready = [arrived[t][steps] for t in later]
        far = down_blocks(after(tuple(hidden), *ready, *moved[0]), w_down[0], far_order)
        ready = [arrived[t][-1] for t in later]
        near = down_blocks(after(tuple(hidden), *far, *ready, *moved[-1]), w_down[0], near_order)
        waits = totals = [pair_sum(n, f, count) for n, f in zip(near, far)]
        moved = [[] for _ in range(steps)]
        before = ()
        for turn, total in zip(turns, totals):
            done, got = gathered_sum(total, count, (before,))
            for step in range(steps):
                moved[step].append(got[step])
            if first + 2 >= parts:
                before = (got[0],)
            if turn:
                back = [((i + turn) % parts, i) for i in range(parts)]
                done = lax.ppermute(done, "exp", back)
            returned.append(done)
    result = residual
    for turn in range(parts):
        numbers = turn * slots + jnp.arange(slots, dtype=jnp.int32)
        weighting = sum(
            jnp.where(slot_of[:, k][:, None] == numbers[None, :], share_of[:, k][:, None], 0.0)
            for k in range(2)
        )
        high = weighting.astype(BF)
        low = (weighting - high.astype(F32)).astype(BF)
        result = result + jnp.dot(high, returned[turn], preferred_element_type=F32)
        result = result + jnp.dot(low, returned[turn], preferred_element_type=F32)
    result = result.astype(BF).reshape(count, tokens, cols)
    blocks = [lax.dynamic_index_in_dim(result, me ^ j, 0, False) for j in range(count)]
    return lay_columns(swap_blocks(blocks, count), mates).reshape(seqs, sub, model)


def solution(mesh):
    return jax.shard_map(
        body,
        mesh=mesh,
        in_specs=(
            P(None, "ctx", "exp"),
            P(None, "ctx", "exp"),
            P(None, "ctx", "exp"),
            P("ctx", "exp"),
            P(None, "ctx", "exp"),
            P("exp"),
            P("exp", "ctx"),
            P(None, ("ctx", "exp"), None),
            P(),
            P(("ctx", "exp"), None, None),
            P(("ctx", "exp"), None, None),
            P("exp", None, "ctx"),
            P("exp", None, "ctx"),
            P("exp", "ctx", None),
        ),
        out_specs=P(None, ("ctx", "exp"), None),
        check_vma=False,
    )
```

time: 540 us -> 467 us (0.86)
  starting transfers between devices: 113 us -> 53.6 us
  local copies, waits for them, and re-layouts: 47.9 us -> 23.6 us
  other arithmetic: 39.2 us -> 16.7 us
  Pallas kernels: 126 us -> 139 us
  between operations: 1.71 us -> 14.6 us
  waiting for transfers between devices: 193 us -> 201 us
    ppermute x18 -> x3, starting transfers between devices: 52.4 us -> 2.11 us  [body(): lax.ppermute(dispatch, 'exp', [(i, (i + turn) % parts) for i in range(par...]
    ppermute x18 -> x3, waiting for transfers between devices: 49.3 us -> 17.9 us  [body(): lax.ppermute(dispatch, 'exp', [(i, (i + turn) % parts) for i in range(par...]
    reduce_scatter x0 -> x2, waiting for transfers between devices: none -> 29.1 us  [body(): summed.append(lax.psum_scatter(partial, 'exp', scatter_dimension=0))]
    unnamed x109 -> x88, local copies, waits for them, and re-layouts: 39.9 us -> 15.1 us
    ppermute x58 -> x70, waiting for transfers between devices: 119 us -> 135 us  [send(): return lax.ppermute(x, 'ctx', perm)]
    concatenate x14 -> x7, other arithmetic: 14.9 us -> 1.55 us  [joined(): return parts[0] if len(parts) == 1 else jnp.concatenate(parts, axis=0)]
    ppermute x58 -> x70, starting transfers between devices: 60 us -> 49.5 us  [send(): return lax.ppermute(x, 'ctx', perm)]
    pallas_call x8 -> x16, Pallas kernels: 107 us -> 117 us  [the longest x2 51.3 us: hidden_units(): pl.pallas_call(functools.partial(hidden_kernel, sizes, many), grid_spec=p...]
  transfers between devices with their start and end apart: 79 -> 78, of which waited for: 40 -> 38; matrix products, arithmetic and copies ran while one was open for 9% -> 6% of each run, Pallas kernels for 23% -> 24%
where the time goes in v2:
time: 467 us; the launch traced here: 459 us
  waiting for transfers between devices  201 us (43%)
  Pallas kernels  139 us (30%)
  starting transfers between devices  53.6 us (11%)
  local copies, waits for them, and re-layouts  23.6 us (5%)
  other arithmetic  16.7 us (4%)
  between operations  14.6 us (3%)
  matrix products  10.5 us (2%)
    ppermute x70, waiting for transfers between devices, send(): return lax.ppermute(x, 'ctx', perm)  135 us
    pallas_call x2, Pallas kernels, hidden_units(): pl.pallas_call(functools.partial(hidden_kernel, sizes, many), grid_spec=p...  51.3 us
    ppermute x70, starting transfers between devices, send(): return lax.ppermute(x, 'ctx', perm)  49.5 us
    pallas_call x4, Pallas kernels, down_blocks(): pl.pallas_call(functools.partial(down_kernel, many), grid_spec=pltpu.Pref...  35.3 us
    reduce_scatter x2, waiting for transfers between devices, body(): summed.append(lax.psum_scatter(partial, 'exp', scatter_dimension=0))  29.1 us
    ppermute x3, waiting for transfers between devices, body(): done = lax.ppermute(done, 'exp', back)  18.6 us
    ppermute x3, waiting for transfers between devices, body(): lax.ppermute(dispatch, 'exp', [(i, (i + turn) % parts) for i in range(par...  17.9 us
    unnamed x88, local copies, waits for them, and re-layouts  15.1 us
  transfers between devices with their start and end apart: 78, of which 38 were waited for; matrix products, arithmetic and copies ran while one was open for 6% of the time, Pallas kernels for 24%

profile of v2, /device:TPU:0, one launch (start us, length us, event | category | flops | bytes accessed | tf_op | source)
XLA Modules:
  0.0 459.1 jit_solution(3433264112248145009)
XLA Ops:
  13.5 4.2 shard_map.137
  17.9 4.2 shard_map.136.refs_0_
  31.9 11.4 %shard_map.139 = (f32[4,64,2048]{2,1,0:T(8,128)}, f32[4,64,2048]{2,1,0:T(8,128)}) custom-call(bf16[4,64,2048]{2,1,0:T(8,128)(2,1)} %q_ref.5, bf16[4,64,2048]{2,1,0:T(8,128)(2,1)} %k_ref.5, bf16[4,64,2048]{2,1,0:T(8,128)(2,1)} %v_ref.5, bf16[4,64,2048]{2,1,0:T(8,128)(2,1)} %g_ref.1, f32[64,16]{1,0:T(8,128)} %copy-done.18, f32[16,64]{1,0:T(8,128)} %bitcast.141, ...), custom_call_target="tpu_custom_call" | custom-call | flops 2013265920 | bytes 8388608 | tf_op jit(solution)/shard_map/pallas_call | solution.py:197
  47.6 13.1 %collective-permute-done.8.refs_2_ = bf16[4,8,128,128]{3,2,1,0:T(8,128)(2,1)} collective-permute-done((bf16[4,8,128,128]{3,2,1,0:T(8,128)(2,1)S(1)}, bf16[4,8,128,128]{3,2,1,0:T(8,128)(2,1)}, u32[]{:S(2)}, u32[]{:S(2)}) %collective-permute-start.8) | collective-permute-done | bytes 1048608 | tf_op jit(solution)/shard_map/ppermute | solution.py:48
  66.9 5.3 %shard_map.143 = bf16[4,2,16,2048]{3,2,1,0:T(8,128)(2,1)} custom-call(s32[1]{0:T(128)} %bitcast.8.place_ref.side_ref, f32[2,16]{1,0:T(2,128)} %stack.67.weight_ref, bf16[4,64,2048]{2,1,0:T(8,128)(2,1)} %q_ref.5, bf16[4,8,128,128]{3,2,1,0:T(8,128)(2,1)} %copy-done.1, bf16[4,8,128,128]{3,2,1,0:T(8,128)(2,1)} %copy-done.34, bf16[4,8,128,128]{3,2,1,0:T(8,128)(2,1)} %copy-done, ...), custom_call_target="tpu_custom_call" | custom-call | flops 6000000000 | bytes 3670016 | tf_op jit(solution)/shard_map/pallas_call | solution.py:269
  73.3 8.4 %collective-permute-done.11.refs_1_ = bf16[1,128,2048]{2,1,0:T(8,128)(2,1)S(1)} collective-permute-done((bf16[1,128,2048]{2,1,0:T(8,128)(2,1)}, bf16[1,128,2048]{2,1,0:T(8,128)(2,1)S(1)}, u32[]{:S(2)}, u32[]{:S(2)}) %collective-permute-start.11) | collective-permute-done | bytes 524320 | tf_op jit(solution)/shard_map/ppermute | solution.py:48
  84.4 13.3 %collective-permute-done.14.refs_2_ = bf16[2,128,2048]{2,1,0:T(8,128)(2,1)S(1)} collective-permute-done((bf16[2,128,2048]{2,1,0:T(8,128)(2,1)S(1)}, bf16[2,128,2048]{2,1,0:T(8,128)(2,1)S(1)}, u32[]{:S(2)}, u32[]{:S(2)}) %collective-permute-start.14) | collective-permute-done | bytes 1048608 | tf_op jit(solution)/shard_map/ppermute | solution.py:48
  98.2 5.3 %shard_map.142 = bf16[4,2,16,2048]{3,2,1,0:T(8,128)(2,1)} custom-call(s32[1]{0:T(128)} %bitcast.8.place_ref.side_ref, f32[2,16]{1,0:T(2,128)} %stack.67.weight_ref, bf16[4,64,2048]{2,1,0:T(8,128)(2,1)} %q_ref.5, bf16[4,8,128,128]{3,2,1,0:T(8,128)(2,1)} %copy-done.1, bf16[4,8,128,128]{3,2,1,0:T(8,128)(2,1)} %copy-done.34, bf16[4,8,128,128]{3,2,1,0:T(8,128)(2,1)} %copy-done, ...), custom_call_target="tpu_custom_call" | custom-call | flops 6000000000 | bytes 3670016 | tf_op jit(solution)/shard_map/pallas_call | solution.py:269
  106.4 5.8 %shard_map.144 = bf16[4,8,32,768]{3,2,1,0:T(8,128)(2,1)} custom-call(s32[8]{0:T(128)S(1)} %stack.66.order_ref, bf16[1,128,2048]{2,1,0:T(8,128)(2,1)S(1)} %bitcast.123, bf16[1,128,2048]{2,1,0:T(8,128)(2,1)S(1)} %collective-permute-done.11.refs_1_, bf16[2,128,2048]{2,1,0:T(8,128)(2,1)S(1)} %collective-permute-done.14.refs_2_, ...), custom_call_target="tpu_custom_call" | custom-call | flops 6442450944 | bytes 8912896 | tf_op jit(solution)/shard_map/pallas_call | solution.py:304
  114.6 13.7 %collective-permute-done.13.refs_2_ = bf16[2,128,2048]{2,1,0:T(8,128)(2,1)S(1)} collective-permute-done((bf16[2,128,2048]{2,1,0:T(8,128)(2,1)S(1)}, bf16[2,128,2048]{2,1,0:T(8,128)(2,1)S(1)}, u32[]{:S(2)}, u32[]{:S(2)}) %collective-permute-start.13) | collective-permute-done | bytes 1048608 | tf_op jit(solution)/shard_map/ppermute | solution.py:48
  134.3 5.1 %shard_map.145 = bf16[4,8,32,768]{3,2,1,0:T(8,128)(2,1)} custom-call(s32[8]{0:T(128)S(1)} %stack.66.order_ref, bf16[1,128,2048]{2,1,0:T(8,128)(2,1)S(1)} %bitcast.119, bf16[1,128,2048]{2,1,0:T(8,128)(2,1)S(1)} %collective-permute-done.12.refs_1_, bf16[2,128,2048]{2,1,0:T(8,128)(2,1)S(1)} %collective-permute-done.13.refs_2_, ...), custom_call_target="tpu_custom_call" | custom-call | flops 6442450944 | bytes 8912896 | tf_op jit(solution)/shard_map/pallas_call | solution.py:304
  150.5 5.4 %collective-permute-done.25.refs_5_ = bf16[64,768]{1,0:T(8,128)(2,1)S(1)} collective-permute-done((bf16[64,768]{1,0:T(8,128)(2,1)}, bf16[64,768]{1,0:T(8,128)(2,1)S(1)}, u32[]{:S(2)}, u32[]{:S(2)}) %collective-permute-start.25) | collective-permute-done | bytes 98336 | tf_op jit(solution)/shard_map/ppermute | solution.py:48
  156.0 29.1 %reduce-scatter.5.cloned.1.call-done = bf16[1,8,32,768]{3,2,1,0:T(8,128)(2,1)} async-done(((bf16[4,8,32,768]{3,2,1,0:T(8,128)(2,1)}), bf16[1,8,32,768]{3,2,1,0:T(8,128)(2,1)}) %reduce-scatter.5.cloned.1.call-update) | async-done | bytes 393232 | tf_op jit(solution)/shard_map/reduce_scatter | solution.py:559
  201.1 5.6 %collective-permute-done.31.refs_1_ = bf16[1,264,768]{2,1,0:T(8,128)(2,1)S(1)} collective-permute-done((bf16[1,264,768]{2,1,0:T(8,128)(2,1)S(1)}, bf16[1,264,768]{2,1,0:T(8,128)(2,1)S(1)}, u32[]{:S(2)}, u32[]{:S(2)}) %collective-permute-start.31) | collective-permute-done | bytes 405536 | tf_op jit(solution)/shard_map/ppermute | solution.py:48
  206.8 4.7 %collective-permute-done.32 = bf16[264,768]{1,0:T(8,128)(2,1)S(1)} collective-permute-done((bf16[264,768]{1,0:T(8,128)(2,1)S(1)}, bf16[264,768]{1,0:T(8,128)(2,1)S(1)}, u32[]{:S(2)}, u32[]{:S(2)}) %collective-permute-start.32) | collective-permute-done | bytes 405536 | tf_op jit(solution)/shard_map/ppermute | solution.py:592
  213.9 10.3 %collective-permute-done.41.refs_7_ = bf16[1,264,768]{2,1,0:T(8,128)(2,1)S(1)} collective-permute-done((bf16[1,264,768]{2,1,0:T(8,128)(2,1)S(1)}, bf16[1,264,768]{2,1,0:T(8,128)(2,1)S(1)}, u32[]{:S(2)}, u32[]{:S(2)}) %collective-permute-start.41) | collective-permute-done | bytes 405536 | tf_op jit(solution)/shard_map/ppermute | solution.py:48
  224.4 5.2 %collective-permute-done.37 = bf16[264,768]{1,0:T(8,128)(2,1)S(1)} collective-permute-done((bf16[264,768]{1,0:T(8,128)(2,1)S(1)}, bf16[264,768]{1,0:T(8,128)(2,1)S(1)}, u32[]{:S(2)}, u32[]{:S(2)}) %collective-permute-start.37) | collective-permute-done | bytes 405536 | tf_op jit(solution)/shard_map/ppermute | solution.py:592
  233.8 8.1 %collective-permute-done.39 = bf16[264,768]{1,0:T(8,128)(2,1)S(1)} collective-permute-done((bf16[264,768]{1,0:T(8,128)(2,1)S(1)}, bf16[264,768]{1,0:T(8,128)(2,1)S(1)}, u32[]{:S(2)}, u32[]{:S(2)}) %collective-permute-start.39) | collective-permute-done | bytes 405536 | tf_op jit(solution)/shard_map/ppermute | solution.py:592
  243.2 4.0 collective-permute-done.42.refs_8_
  254.8 25.9 %shard_map.148 = (bf16[264,1152]{1,0:T(8,128)(2,1)}, bf16[264,1152]{1,0:T(8,128)(2,1)}) custom-call(s32[8]{0:T(128)} %copy-done.8, bf16[1,264,768]{2,1,0:T(8,128)(2,1)} %copy-done.23, bf16[1,264,768]{2,1,0:T(8,128)(2,1)} %copy-done.24, bf16[2,264,768]{2,1,0:T(8,128)(2,1)} %copy-done.35, bf16[1,264,768]{2,1,0:T(8,128)(2,1)} %copy-done.39, ...), custom_call_target="tpu_custom_call" | custom-call | flops 29896998912 | bytes 34799616 | tf_op jit(solution)/shard_map/pallas_call | solution.py:398
  280.7 8.9 %shard_map.149 = (bf16[4,264,768]{2,1,0:T(8,128)(2,1)}, bf16[4,264,768]{2,1,0:T(8,128)(2,1)}) custom-call(s32[4]{0:T(128)} %pad_add_fusion.1.order_ref, bf16[264,1152]{1,0:T(8,128)(2,1)} %get-tuple-element.102.refs_0_, bf16[264,1152]{1,0:T(8,128)(2,1)} %get-tuple-element.103.refs_1_, bf16[1152,6144]{1,0:T(8,128)(2,1)} %bitcast.146), custom_call_target="tpu_custom_call" | custom-call | flops 7474249728 | bytes 10321920 | tf_op jit(solution)/shard_map/pallas_call | solution.py:430
  291.3 3.6 collective-permute-done.48.refs_5_
  296.5 8.7 %shard_map.150 = (bf16[4,264,768]{2,1,0:T(8,128)(2,1)}, bf16[4,264,768]{2,1,0:T(8,128)(2,1)}) custom-call(s32[4]{0:T(128)} %pad_add_fusion.order_ref, bf16[264,1152]{1,0:T(8,128)(2,1)} %get-tuple-element.102.refs_0_, bf16[264,1152]{1,0:T(8,128)(2,1)} %get-tuple-element.103.refs_1_, bf16[1152,6144]{1,0:T(8,128)(2,1)} %bitcast.147), custom_call_target="tpu_custom_call" | custom-call | flops 7474249728 | bytes 10321920 | tf_op jit(solution)/shard_map/pallas_call | solution.py:430
  316.6 25.4 %shard_map.151 = (bf16[264,1152]{1,0:T(8,128)(2,1)}, bf16[264,1152]{1,0:T(8,128)(2,1)}) custom-call(s32[8]{0:T(128)} %copy-done.8, bf16[1,264,768]{2,1,0:T(8,128)(2,1)} %bitcast.131, bf16[1,264,768]{2,1,0:T(8,128)(2,1)} %copy-done.21, bf16[2,264,768]{2,1,0:T(8,128)(2,1)} %collective-permute-done.46.refs_2_, ...), custom_call_target="tpu_custom_call" | custom-call | flops 29896998912 | bytes 34799616 | tf_op jit(solution)/shard_map/pallas_call | solution.py:398
  342.0 8.9 %shard_map.152 = (bf16[4,264,768]{2,1,0:T(8,128)(2,1)}, bf16[4,264,768]{2,1,0:T(8,128)(2,1)}) custom-call(s32[4]{0:T(128)} %pad_add_fusion.1.order_ref, bf16[264,1152]{1,0:T(8,128)(2,1)} %get-tuple-element.118.refs_0_, bf16[264,1152]{1,0:T(8,128)(2,1)} %get-tuple-element.119.refs_1_, bf16[1152,6144]{1,0:T(8,128)(2,1)} %bitcast.148), custom_call_target="tpu_custom_call" | custom-call | flops 7474249728 | bytes 10321920 | tf_op jit(solution)/shard_map/pallas_call | solution.py:430
  360.6 4.2 collective-permute-done.55
  364.8 8.7 %shard_map.153 = (bf16[4,264,768]{2,1,0:T(8,128)(2,1)}, bf16[4,264,768]{2,1,0:T(8,128)(2,1)}) custom-call(s32[4]{0:T(128)} %pad_add_fusion.order_ref, bf16[264,1152]{1,0:T(8,128)(2,1)} %get-tuple-element.118.refs_0_, bf16[264,1152]{1,0:T(8,128)(2,1)} %get-tuple-element.119.refs_1_, bf16[1152,6144]{1,0:T(8,128)(2,1)} %bitcast.149), custom_call_target="tpu_custom_call" | custom-call | flops 7474249728 | bytes 10321920 | tf_op jit(solution)/shard_map/pallas_call | solution.py:430
  382.8 5.4 %collective-permute-done.62 = bf16[2,264,768]{2,1,0:T(8,128)(2,1)S(1)} collective-permute-done((bf16[2,264,768]{2,1,0:T(8,128)(2,1)S(1)}, bf16[2,264,768]{2,1,0:T(8,128)(2,1)S(1)}, u32[]{:S(2)}, u32[]{:S(2)}) %collective-permute-start.62) | collective-permute-done | bytes 811040 | tf_op jit(solution)/shard_map/ppermute | solution.py:48
  393.2 11.8 %collective-permute-done.66 = bf16[2,264,768]{2,1,0:T(8,128)(2,1)S(1)} collective-permute-done((bf16[2,264,768]{2,1,0:T(8,128)(2,1)S(1)}, bf16[2,264,768]{2,1,0:T(8,128)(2,1)S(1)}, u32[]{:S(2)}, u32[]{:S(2)}) %collective-permute-start.66) | collective-permute-done | bytes 811040 | tf_op jit(solution)/shard_map/ppermute | solution.py:48
  407.0 6.3 %collective-permute-done.67 = bf16[1,264,768]{2,1,0:T(8,128)(2,1)S(1)} collective-permute-done((bf16[1,264,768]{2,1,0:T(8,128)(2,1)S(1)}, bf16[1,264,768]{2,1,0:T(8,128)(2,1)S(1)}, u32[]{:S(2)}, u32[]{:S(2)}) %collective-permute-start.67) | collective-permute-done | bytes 405536 | tf_op jit(solution)/shard_map/ppermute | solution.py:48
  413.5 18.6 %collective-permute-done.64 = bf16[264,768]{1,0:T(8,128)(2,1)S(1)} collective-permute-done((bf16[264,768]{1,0:T(8,128)(2,1)S(1)}, bf16[264,768]{1,0:T(8,128)(2,1)S(1)}, u32[]{:S(2)}, u32[]{:S(2)}) %collective-permute-start.64) | collective-permute-done | bytes 405536 | tf_op jit(solution)/shard_map/ppermute | solution.py:631
  443.9 5.1 %collective-permute-done.73.refs_5_ = bf16[64,768]{1,0:T(8,128)(2,1)S(1)} collective-permute-done((bf16[64,768]{1,0:T(8,128)(2,1)S(1)}, bf16[64,768]{1,0:T(8,128)(2,1)S(1)}, u32[]{:S(2)}, u32[]{:S(2)}) %collective-permute-start.73) | collective-permute-done | bytes 98336 | tf_op jit(solution)/shard_map/ppermute | solution.py:48
  (331 shorter events, 140.7 us)
Async XLA Ops:
  6.5 149.5 %reduce-scatter.3.cloned.1.call-start = ((), (), s32[]{:S(2)}) async-start(), calls=%async_computation.2 | async-start | bytes 1966080 | tf_op jit(solution)/shard_map/reduce_scatter | solution.py:559
  9.3 12.9 %collective-permute-start.1 = (f32[1,3,128]{2,1,0:T(4,128)S(1)}, f32[1,3,128]{2,1,0:T(4,128)S(1)}, u32[]{:S(2)}, u32[]{:S(2)}) collective-permute-start(f32[1,3,128]{2,1,0:T(4,128)S(1)} %get-tuple-element.144), channel_id=1, source_target_pairs={{0,8},{4,20},{8,0},{12,28},{16,24},{20,4},{24,16},{28,12},{1,9},{5... | collective-permute-start | bytes 4616 | tf_op jit(solution)/shard_map/ppermute | solution.py:48
  12.3 13.7 %collective-permute-start.3 = (f32[1,3,128]{2,1,0:T(4,128)S(1)}, f32[1,3,128]{2,1,0:T(4,128)S(1)}, u32[]{:S(2)}, u32[]{:S(2)}) collective-permute-start(f32[1,3,128]{2,1,0:T(4,128)S(1)} %get-tuple-element.144), channel_id=1, source_target_pairs={{0,4},{4,0},{8,12},{12,8},{16,20},{20,16},{24,28},{28,24},{1,5},{5... | collective-permute-start | bytes 4616 | tf_op jit(solution)/shard_map/ppermute | solution.py:48
  29.9 14.9 %collective-permute-start.7 = (bf16[1,4,8,128,128]{4,3,2,1,0:T(8,128)(2,1)S(1)}, bf16[1,4,8,128,128]{4,3,2,1,0:T(8,128)(2,1)S(1)}, u32[]{:S(2)}, u32[]{:S(2)}) collective-permute-start(bf16[1,4,8,128,128]{4,3,2,1,0:T(8,128)(2,1)S(1)} %bitcast.113), channel_id=1, source_target_pairs={{0,8},{4,20},{8,0},{12,28},{16,24},{20,4},{24,16},{28,12},{1,9},{5... | collective-permute-start | bytes 3145736 | tf_op jit(solution)/shard_map/ppermute | solution.py:48
  45.8 15.0 %collective-permute-start.8 = (bf16[4,8,128,128]{3,2,1,0:T(8,128)(2,1)S(1)}, bf16[4,8,128,128]{3,2,1,0:T(8,128)(2,1)}, u32[]{:S(2)}, u32[]{:S(2)}) collective-permute-start(bf16[4,8,128,128]{3,2,1,0:T(8,128)(2,1)S(1)} %shard_map.140), channel_id=1, source_target_pairs={{0,16},{4,12},{8,24},{12,4},{16,0},{20,28},{24,8},{28,20},{1,17},{... | collective-permute-start | bytes 3145736 | tf_op jit(solution)/shard_map/ppermute | solution.py:48
  47.4 16.6 %collective-permute-start.10 = (bf16[4,8,128,128]{3,2,1,0:T(8,128)(2,1)}, bf16[4,8,128,128]{3,2,1,0:T(8,128)(2,1)}, u32[]{:S(2)}, u32[]{:S(2)}) collective-permute-start(bf16[4,8,128,128]{3,2,1,0:T(8,128)(2,1)} %shard_map.136.refs_0_), channel_id=1, source_target_pairs={{0,4},{4,0},{8,12},{12,8},{16,20},{20,16},{24,28},{28,24},{1,5},{5... | collective-permute-start | bytes 3145736 | tf_op jit(solution)/shard_map/ppermute | solution.py:48
  82.8 14.9 %collective-permute-start.14 = (bf16[2,128,2048]{2,1,0:T(8,128)(2,1)S(1)}, bf16[2,128,2048]{2,1,0:T(8,128)(2,1)S(1)}, u32[]{:S(2)}, u32[]{:S(2)}) collective-permute-start(bf16[2,128,2048]{2,1,0:T(8,128)(2,1)S(1)} %pad_maximum_fusion.1), channel_id=1, source_target_pairs={{0,16},{4,12},{8,24},{12,4},{16,0},{20,28},{24,8},{28,20},{1,17},{... | collective-permute-start | bytes 3145736 | tf_op jit(solution)/shard_map/ppermute | solution.py:48
  112.3 72.8 %reduce-scatter.5.cloned.1.call-start = ((), (), s32[]{:S(2)}) async-start(), calls=%async_computation.3 | async-start | bytes 1966080 | tf_op jit(solution)/shard_map/reduce_scatter | solution.py:559
  113.4 14.9 %collective-permute-start.13 = (bf16[2,128,2048]{2,1,0:T(8,128)(2,1)S(1)}, bf16[2,128,2048]{2,1,0:T(8,128)(2,1)S(1)}, u32[]{:S(2)}, u32[]{:S(2)}) collective-permute-start(bf16[2,128,2048]{2,1,0:T(8,128)(2,1)S(1)} %pad_maximum_fusion), channel_id=1, source_target_pairs={{0,16},{4,12},{8,24},{12,4},{16,0},{20,28},{24,8},{28,20},{1,17},{... | collective-permute-start | bytes 3145736 | tf_op jit(solution)/shard_map/ppermute | solution.py:48
  211.4 18.1 %collective-permute-start.33 = (bf16[2,264,768]{2,1,0:T(8,128)(2,1)S(1)}, bf16[2,264,768]{2,1,0:T(8,128)(2,1)S(1)}, u32[]{:S(2)}, u32[]{:S(2)}) collective-permute-start(bf16[2,264,768]{2,1,0:T(8,128)(2,1)S(1)} %pad_maximum_fusion.2), channel_id=1, source_target_pairs={{0,16},{4,12},{8,24},{12,4},{16,0},{20,28},{24,8},{28,20},{1,17},{... | collective-permute-start | bytes 2433032 | tf_op jit(solution)/shard_map/ppermute | solution.py:48
  212.0 12.3 %collective-permute-start.41 = (bf16[1,264,768]{2,1,0:T(8,128)(2,1)S(1)}, bf16[1,264,768]{2,1,0:T(8,128)(2,1)S(1)}, u32[]{:S(2)}, u32[]{:S(2)}) collective-permute-start(bf16[1,264,768]{2,1,0:T(8,128)(2,1)S(1)} %bitcast.136), channel_id=1, source_target_pairs={{0,8},{4,20},{8,0},{12,28},{16,24},{20,4},{24,16},{28,12},{1,9},{5... | collective-permute-start | bytes 1216520 | tf_op jit(solution)/shard_map/ppermute | solution.py:48
  213.9 15.7 %collective-permute-start.37 = (bf16[264,768]{1,0:T(8,128)(2,1)S(1)}, bf16[264,768]{1,0:T(8,128)(2,1)S(1)}, u32[]{:S(2)}, u32[]{:S(2)}) collective-permute-start(bf16[264,768]{1,0:T(8,128)(2,1)S(1)} %convolution_convert_fusion.1), channel_id=1, source_target_pairs={{0,2},{1,3},{2,0},{3,1},{4,6},{5,7},{6,4},{7,5},{8,10},{9,11},{10,... | collective-permute-start | bytes 1216520 | tf_op jit(solution)/shard_map/ppermute | solution.py:592
  229.6 17.6 %collective-permute-start.42 = (bf16[2,264,768]{2,1,0:T(8,128)(2,1)S(1)}, bf16[2,264,768]{2,1,0:T(8,128)(2,1)S(1)}, u32[]{:S(2)}, u32[]{:S(2)}) collective-permute-start(bf16[2,264,768]{2,1,0:T(8,128)(2,1)S(1)} %pad_maximum_fusion.3), channel_id=1, source_target_pairs={{0,16},{4,12},{8,24},{12,4},{16,0},{20,28},{24,8},{28,20},{1,17},{... | collective-permute-start | bytes 2433032 | tf_op jit(solution)/shard_map/ppermute | solution.py:48
  233.4 13.7 %collective-permute-start.34 = (bf16[1,264,768]{2,1,0:T(8,128)(2,1)S(1)}, bf16[1,264,768]{2,1,0:T(8,128)(2,1)S(1)}, u32[]{:S(2)}, u32[]{:S(2)}) collective-permute-start(bf16[1,264,768]{2,1,0:T(8,128)(2,1)S(1)} %fusion.10.refs_0_), channel_id=1, source_target_pairs={{0,4},{4,0},{8,12},{12,8},{16,20},{20,16},{24,28},{28,24},{1,5},{5... | collective-permute-start | bytes 1216520 | tf_op jit(solution)/shard_map/ppermute | solution.py:48
  233.4 14.3 %collective-permute-start.38 = (bf16[1,264,768]{2,1,0:T(8,128)(2,1)S(1)}, bf16[1,264,768]{2,1,0:T(8,128)(2,1)S(1)}, u32[]{:S(2)}, u32[]{:S(2)}) collective-permute-start(bf16[1,264,768]{2,1,0:T(8,128)(2,1)S(1)} %bitcast.128), channel_id=1, source_target_pairs={{0,8},{4,20},{8,0},{12,28},{16,24},{20,4},{24,16},{28,12},{1,9},{5... | collective-permute-start | bytes 1216520 | tf_op jit(solution)/shard_map/ppermute | solution.py:48
  251.2 29.5 %collective-permute-start.46 = (bf16[2,264,768]{2,1,0:T(8,128)(2,1)S(1)}, bf16[2,264,768]{2,1,0:T(8,128)(2,1)}, u32[]{:S(2)}, u32[]{:S(2)}) collective-permute-start(bf16[2,264,768]{2,1,0:T(8,128)(2,1)S(1)} %pad_maximum_fusion.4), channel_id=1, source_target_pairs={{0,16},{4,12},{8,24},{12,4},{16,0},{20,28},{24,8},{28,20},{1,17},{... | collective-permute-start | bytes 2433032 | tf_op jit(solution)/shard_map/ppermute | solution.py:48
  253.0 27.7 %collective-permute-start.47 = (bf16[2,264,768]{2,1,0:T(8,128)(2,1)S(1)}, bf16[2,264,768]{2,1,0:T(8,128)(2,1)}, u32[]{:S(2)}, u32[]{:S(2)}) collective-permute-start(bf16[2,264,768]{2,1,0:T(8,128)(2,1)S(1)} %pad_maximum_fusion.5), channel_id=1, source_target_pairs={{0,16},{4,12},{8,24},{12,4},{16,0},{20,28},{24,8},{28,20},{1,17},{... | collective-permute-start | bytes 2433032 | tf_op jit(solution)/shard_map/ppermute | solution.py:48
  289.7 15.6 %collective-permute-start.50 = (bf16[4,264,768]{2,1,0:T(8,128)(2,1)}, bf16[4,264,768]{2,1,0:T(8,128)(2,1)S(1)}, u32[]{:S(2)}, u32[]{:S(2)}) collective-permute-start(bf16[4,264,768]{2,1,0:T(8,128)(2,1)} %get-tuple-element.100), channel_id=1, source_target_pairs={{0,4},{4,0},{8,12},{12,8},{16,20},{20,16},{24,28},{28,24},{1,5},{5... | collective-permute-start | bytes 4866056 | tf_op jit(solution)/shard_map/ppermute | solution.py:48
  290.2 19.6 %collective-permute-start.53 = (bf16[4,264,768]{2,1,0:T(8,128)(2,1)}, bf16[4,264,768]{2,1,0:T(8,128)(2,1)}, u32[]{:S(2)}, u32[]{:S(2)}) collective-permute-start(bf16[4,264,768]{2,1,0:T(8,128)(2,1)} %get-tuple-element.101), channel_id=1, source_target_pairs={{0,4},{4,0},{8,12},{12,8},{16,20},{20,16},{24,28},{28,24},{1,5},{5... | collective-permute-start | bytes 4866056 | tf_op jit(solution)/shard_map/ppermute | solution.py:48
  291.3 23.2 %collective-permute-start.57 = (bf16[1,264,768]{2,1,0:T(8,128)(2,1)S(1)}, bf16[1,264,768]{2,1,0:T(8,128)(2,1)}, u32[]{:S(2)}, u32[]{:S(2)}) collective-permute-start(bf16[1,264,768]{2,1,0:T(8,128)(2,1)S(1)} %bitcast.130), channel_id=1, source_target_pairs={{0,4},{4,0},{8,12},{12,8},{16,20},{20,16},{24,28},{28,24},{1,5},{5... | collective-permute-start | bytes 1216520 | tf_op jit(solution)/shard_map/ppermute | solution.py:48
  294.9 21.7 %collective-permute-start.59 = (bf16[1,264,768]{2,1,0:T(8,128)(2,1)}, bf16[1,264,768]{2,1,0:T(8,128)(2,1)}, u32[]{:S(2)}, u32[]{:S(2)}) collective-permute-start(bf16[1,264,768]{2,1,0:T(8,128)(2,1)} %bitcast.134), channel_id=1, source_target_pairs={{0,4},{4,0},{8,12},{12,8},{16,20},{20,16},{24,28},{28,24},{1,5},{5... | collective-permute-start | bytes 1216520 | tf_op jit(solution)/shard_map/ppermute | solution.py:48
  296.4 18.1 %collective-permute-start.58 = (bf16[1,264,768]{2,1,0:T(8,128)(2,1)}, bf16[1,264,768]{2,1,0:T(8,128)(2,1)}, u32[]{:S(2)}, u32[]{:S(2)}) collective-permute-start(bf16[1,264,768]{2,1,0:T(8,128)(2,1)} %copy-done.21), channel_id=1, source_target_pairs={{0,4},{4,0},{8,12},{12,8},{16,20},{20,16},{24,28},{28,24},{1,5},{5... | collective-permute-start | bytes 1216520 | tf_op jit(solution)/shard_map/ppermute | solution.py:48
  314.5 27.5 %collective-permute-start.51 = (bf16[2,264,768]{2,1,0:T(8,128)(2,1)}, bf16[2,264,768]{2,1,0:T(8,128)(2,1)}, u32[]{:S(2)}, u32[]{:S(2)}) collective-permute-start(bf16[2,264,768]{2,1,0:T(8,128)(2,1)} %slice.135), channel_id=1, source_target_pairs={{0,16},{4,12},{8,24},{12,4},{16,0},{20,28},{24,8},{28,20},{1,17},{... | collective-permute-start | bytes 2433032 | tf_op jit(solution)/shard_map/ppermute | solution.py:48
  315.9 26.1 %collective-permute-start.54 = (bf16[2,264,768]{2,1,0:T(8,128)(2,1)}, bf16[2,264,768]{2,1,0:T(8,128)(2,1)}, u32[]{:S(2)}, u32[]{:S(2)}) collective-permute-start(bf16[2,264,768]{2,1,0:T(8,128)(2,1)} %slice.139), channel_id=1, source_target_pairs={{0,16},{4,12},{8,24},{12,4},{16,0},{20,28},{24,8},{28,20},{1,17},{... | collective-permute-start | bytes 2433032 | tf_op jit(solution)/shard_map/ppermute | solution.py:48
  351.0 22.6 %collective-permute-start.61 = (bf16[4,264,768]{2,1,0:T(8,128)(2,1)}, bf16[4,264,768]{2,1,0:T(8,128)(2,1)}, u32[]{:S(2)}, u32[]{:S(2)}) collective-permute-start(bf16[4,264,768]{2,1,0:T(8,128)(2,1)} %get-tuple-element.116), channel_id=1, source_target_pairs={{0,4},{4,0},{8,12},{12,8},{16,20},{20,16},{24,28},{28,24},{1,5},{5... | collective-permute-start | bytes 4866056 | tf_op jit(solution)/shard_map/ppermute | solution.py:48
  356.9 24.0 %collective-permute-start.65 = (bf16[4,264,768]{2,1,0:T(8,128)(2,1)}, bf16[4,264,768]{2,1,0:T(8,128)(2,1)}, u32[]{:S(2)}, u32[]{:S(2)}) collective-permute-start(bf16[4,264,768]{2,1,0:T(8,128)(2,1)} %get-tuple-element.117), channel_id=1, source_target_pairs={{0,4},{4,0},{8,12},{12,8},{16,20},{20,16},{24,28},{28,24},{1,5},{5... | collective-permute-start | bytes 4866056 | tf_op jit(solution)/shard_map/ppermute | solution.py:48
  375.9 12.3 %collective-permute-start.62 = (bf16[2,264,768]{2,1,0:T(8,128)(2,1)S(1)}, bf16[2,264,768]{2,1,0:T(8,128)(2,1)S(1)}, u32[]{:S(2)}, u32[]{:S(2)}) collective-permute-start(bf16[2,264,768]{2,1,0:T(8,128)(2,1)S(1)} %slice.143), channel_id=1, source_target_pairs={{0,16},{4,12},{8,24},{12,4},{16,0},{20,28},{24,8},{28,20},{1,17},{... | collective-permute-start | bytes 2433032 | tf_op jit(solution)/shard_map/ppermute | solution.py:48
  377.5 15.0 %collective-permute-start.56 = (bf16[264,768]{1,0:T(8,128)(2,1)S(1)}, bf16[264,768]{1,0:T(8,128)(2,1)S(1)}, u32[]{:S(2)}, u32[]{:S(2)}) collective-permute-start(bf16[264,768]{1,0:T(8,128)(2,1)S(1)} %fusion.29), channel_id=1, source_target_pairs={{1,0},{2,1},{3,2},{0,3},{5,4},{6,5},{7,6},{4,7},{9,8},{10,9},{11,1... | collective-permute-start | bytes 1216520 | tf_op jit(solution)/shard_map/ppermute | solution.py:631
  388.2 16.9 %collective-permute-start.66 = (bf16[2,264,768]{2,1,0:T(8,128)(2,1)S(1)}, bf16[2,264,768]{2,1,0:T(8,128)(2,1)S(1)}, u32[]{:S(2)}, u32[]{:S(2)}) collective-permute-start(bf16[2,264,768]{2,1,0:T(8,128)(2,1)S(1)} %slice.147), channel_id=1, source_target_pairs={{0,16},{4,12},{8,24},{12,4},{16,0},{20,28},{24,8},{28,20},{1,17},{... | collective-permute-start | bytes 2433032 | tf_op jit(solution)/shard_map/ppermute | solution.py:48
  391.6 14.4 %collective-permute-start.63 = (bf16[1,264,768]{2,1,0:T(8,128)(2,1)S(1)}, bf16[1,264,768]{2,1,0:T(8,128)(2,1)S(1)}, u32[]{:S(2)}, u32[]{:S(2)}) collective-permute-start(bf16[1,264,768]{2,1,0:T(8,128)(2,1)S(1)} %slice.145), channel_id=1, source_target_pairs={{0,8},{4,20},{8,0},{12,28},{16,24},{20,4},{24,16},{28,12},{1,9},{5... | collective-permute-start | bytes 1216520 | tf_op jit(solution)/shard_map/ppermute | solution.py:48
  406.2 25.8 %collective-permute-start.64 = (bf16[264,768]{1,0:T(8,128)(2,1)S(1)}, bf16[264,768]{1,0:T(8,128)(2,1)S(1)}, u32[]{:S(2)}, u32[]{:S(2)}) collective-permute-start(bf16[264,768]{1,0:T(8,128)(2,1)S(1)} %fusion.30), channel_id=1, source_target_pairs={{2,0},{3,1},{0,2},{1,3},{6,4},{7,5},{4,6},{5,7},{10,8},{11,9},{8,1... | collective-permute-start | bytes 1216520 | tf_op jit(solution)/shard_map/ppermute | solution.py:631
  413.4 20.1 %collective-permute-start.68 = (bf16[264,768]{1,0:T(8,128)(2,1)S(1)}, bf16[264,768]{1,0:T(8,128)(2,1)S(1)}, u32[]{:S(2)}, u32[]{:S(2)}) collective-permute-start(bf16[264,768]{1,0:T(8,128)(2,1)S(1)} %fusion.31), channel_id=1, source_target_pairs={{3,0},{0,1},{1,2},{2,3},{7,4},{4,5},{5,6},{6,7},{11,8},{8,9},{9,10... | collective-permute-start | bytes 1216520 | tf_op jit(solution)/shard_map/ppermute | solution.py:631
  (89 other events, 788.2 us)
Sparse Core Ops, SparseCore 0:
  112.4 36.0 reduce-scatter.2
  150.8 34.2 reduce-scatter.4
